TPU v7x, 256 devices: a whole 4x4x8 slice. The times are simulated.
256 devices in a mesh: tm: 8 (over z), rows: 32 (over x, y, core).
Axes of the slice: x: 4, y: 4, z: 8, core: 2. Of those that a mesh axis runs over, the one named last changes fastest.
Arguments:
- misfit: float32 [8, 8, 512, 1024], P('tm', None, 'rows'), may hold values from -6 to 6
- multiplier_start: float32 [8, 8, 512, 1024], P('tm', None, 'rows'), may hold values from -4 to 4
- increment_start: float32 [8, 8, 512, 1024], P('tm', None, 'rows'), may hold values from -4 to 4
- obs_values: float32 [8, 8, 16384], P('tm', None, 'rows'), may hold values from -6 to 6
- obs_weights: float32 [8, 8, 16384], P('tm', None, 'rows'), may hold values from 0.5 to 2
- obs_cells: int32 [8, 16384], P('tm', 'rows'), may hold values from 0 to 16383
- wind_table: float32 [4, 2, 512, 1024], P(None, None, 'rows'), may hold values from -0.3 to 0.3
- wind_choice: int32 [8, 8], replicated, may hold values from 0 to 3
- spectrum: float32 [8, 512, 1024], P(None, None, 'rows'), may hold values from 0.2 to 2
Outputs:
- multiplier: float32 [8, 8, 512, 1024], P('tm', None, 'rows')
- increment: float32 [8, 8, 512, 1024], P('tm', None, 'rows')
Inputs may be any that keep to these rules, and one draw needn't show every extreme that they name: obs_cells counts cells of the 16 x 1024 block of rows that holds its block of 512 observations; cells may repeat.
All inputs are finite; a program needn't handle non-finite values.
Results may differ from a plain program's by a relative error of at most 0.0001.
Values sent between devices are 32-bit elements; how exact they have to be, the bound alone decides.
A program may use at most 128 MiB of HBM per device.

v0:
```python
import math

import jax
import jax.numpy as jnp
from jax import lax
from jax.sharding import PartitionSpec as P

ITERS = 2


NU = 0.12
HIGH = lax.Precision.HIGHEST


def with_halo(cells, sides, width):
    for axis, dim in sides:
        count = lax.axis_size(axis)
        head = lax.slice_in_dim(cells, 0, width, axis=dim)
        tail = lax.slice_in_dim(cells, cells.shape[dim] - width, cells.shape[dim], axis=dim)
        cells = jnp.concatenate(
            [
                lax.ppermute(tail, axis, [(i, (i + 1) % count) for i in range(count)]),
                cells,
                lax.ppermute(head, axis, [((i + 1) % count, i) for i in range(count)]),
            ],
            axis=dim,
        )
    return cells


def from_behind(block, axis, distance):
    devices = range(lax.axis_size(axis))
    route = [(i - distance, i) for i in devices if i - distance in devices]
    return lax.ppermute(block, axis, route)


def cas_table(length):
    count = lax.iota(jnp.int32, length)
    phase = count[:, None] * count[None, :] % length
    angle = phase.astype(jnp.float32) * (2.0 * math.pi / length)
    return jnp.cos(angle) + jnp.sin(angle)


def trimmed(padded, have, want):
    cut = have - want
    return lax.slice_in_dim(padded, cut, padded.shape[-2] - cut, axis=padded.ndim - 2)


def forward_step(padded, east_wind, north_wind):
    center = padded[:, 1:-1]
    north = padded[:, 2:]
    south = padded[:, :-2]
    east = jnp.roll(center, -1, 2)
    west = jnp.roll(center, 1, 2)
    drift = east_wind[:, 1:-1] * (east - west) + north_wind[:, 1:-1] * (north - south)
    return center + NU * (east + west + north + south - 4.0 * center) - 0.5 * drift


def adjoint_step(padded, east_wind, north_wind):
    center = padded[:, 1:-1]
    north = padded[:, 2:]
    south = padded[:, :-2]
    east = jnp.roll(center, -1, 2)
    west = jnp.roll(center, 1, 2)
    along = east_wind[:, 1:-1] * center
    across = north_wind * padded
    spread = jnp.roll(along, -1, 2) - jnp.roll(along, 1, 2) + across[:, 2:] - across[:, :-2]
    return center + NU * (east + west + north + south - 4.0 * center) + 0.5 * spread


def propagate(field, winds, stepper):
    result = field
    for repeat in range(2):
        padded = with_halo(result, (("rows", 1),), 1)
        result = stepper(padded, trimmed(winds[:, 0], 2, 1), trimmed(winds[:, 1], 2, 1))
    return result


def covariance(field, spectrum_cols, table_x, table_y):
    column_side = jnp.einsum("lrx,xk->lkr", field, table_x, precision=HIGH)
    columns = lax.all_to_all(column_side, "rows", split_axis=1, concat_axis=2, tiled=True)
    spectral = jnp.einsum("lcy,yk->lck", columns, table_y, precision=HIGH) * spectrum_cols
    returned = jnp.einsum("lck,ky->lcy", spectral, table_y, precision=HIGH)
    row_again = lax.all_to_all(returned, "rows", split_axis=2, concat_axis=1, tiled=True)
    whole = table_x.shape[0] * table_y.shape[0]
    return jnp.einsum("lkr,kx->lrx", row_again, table_x, precision=HIGH) / whole


def on_device(
    misfit,
    multiplier_start,
    increment_start,
    obs_values,
    obs_weights,
    obs_cells,
    wind_table,
    wind_choice,
    spectrum,
):
    target = misfit[0]
    multiplier = multiplier_start[0]
    increment = increment_start[0]
    levels, rows_dev, width = multiplier.shape
    sections = wind_choice.shape[0]
    here = lax.axis_index("tm")
    before = (here + sections - 1) % sections
    picks = jnp.stack(
        [
            lax.dynamic_index_in_dim(wind_choice, here, 0, keepdims=False),
            lax.dynamic_index_in_dim(wind_choice, before, 0, keepdims=False),
        ]
    )
    matches = picks[:, :, None] == lax.iota(jnp.int32, wind_table.shape[0])[None, None, :]
    chosen = jnp.sum(
        jnp.where(matches[:, :, :, None, None, None], wind_table[None, None], 0.0), axis=2
    )
    padded_winds = with_halo(chosen, (("rows", 3),), 2)
    wind_own = padded_winds[0]
    wind_prev = padded_winds[1]
    table_x = cas_table(width)
    table_y = cas_table(rows_dev * lax.axis_size("rows"))
    spectrum_cols = jnp.transpose(spectrum, (0, 2, 1))
    cells = obs_cells[0]
    observed = obs_values[0]
    weights = obs_weights[0]
    for step in range(ITERS):
        filtered = covariance(multiplier, spectrum_cols, table_x, table_y)
        forward = propagate(from_behind(increment, "tm", 1), wind_prev, forward_step)
        r_lam = target - filtered - increment + forward
        total_lam = lax.psum(jnp.sum(r_lam * r_lam), ("tm", "rows"))
        flat = increment.reshape(levels, rows_dev * width)
        picked = jnp.take(flat, cells, axis=1)
        weighted = weights * (observed - picked)
        spread = jnp.zeros((levels, rows_dev * width), jnp.float32).at[:, cells].add(weighted)
        spread = spread.reshape(levels, rows_dev, width)
        backward = propagate(from_behind(multiplier, "tm", -1), wind_own, adjoint_step)
        r_dx = spread - multiplier + backward
        total_dx = lax.psum(jnp.sum(r_dx * r_dx), ("tm", "rows"))
        theta = total_lam / (total_lam + total_dx + 1e-06)
        multiplier = multiplier + theta * r_lam
        increment = increment + (1.0 - theta) * r_dx
    return (multiplier[None], increment[None])


def solution(mesh):
    return jax.shard_map(
        on_device,
        mesh=mesh,
        in_specs=(
            P("tm", None, "rows", None),
            P("tm", None, "rows", None),
            P("tm", None, "rows", None),
            P("tm", None, "rows"),
            P("tm", None, "rows"),
            P("tm", "rows"),
            P(None, None, "rows", None),
            P(),
            P(None, None, "rows"),
        ),
        out_specs=(P("tm", None, "rows", None), P("tm", None, "rows", None)),
        check_vma=False,
    )
```

profile of v0, /device:TPU:1, one launch (start us, length us, event | category | flops | bytes accessed | tf_op | source)
XLA Modules:
  0.0 511.7 jit_solution(12946320178042314087)
XLA Ops:
  1.5 2.4 select_reduce_fusion
  4.9 2.7 collective-permute-start.3
  8.2 1.3 collective-permute-start.7
  9.5 4.8 collective-permute-start
  14.3 21.4 %fusion.18 = f32[8,1024,16]{1,2,0:T(8,128)} fusion(f32[1,8,16,1024]{3,2,1,0:T(8,128)} %param.12), kind=kOutput, calls=%fused_computation.35 | convolution fusion | flops 1626341376 | bytes 1048576 | tf_op jit(solution)/shard_map/lrx,xk->lkr/dot_general | solution.py:80
  35.6 3.6 copy.49
  39.2 4.2 reshape.114
  43.4 10.3 %all-to-all-start = ((f32[32,1,4096]{2,1,0:T(1,128)}), f32[32,1,4096]{2,1,0:T(1,128)}, u32[]{:S(2)}, u32[]{:S(2)}) async-start(f32[32,1,4096]{2,1,0:T(1,128)} %reshape.114), calls=%async_computation | async-start | bytes 1048576 | tf_op jit(solution)/shard_map/all_to_all | solution.py:81
  53.9 4.7 copy.60
  58.8 9.0 %scatter_custom_fusion = f32[8,16384]{0,1:T(8,128)} fusion(s32[512]{0:T(512)S(1)} %bitcast.182, f32[]{:T(128)} %constant.85.clone.1, f32[1,8,512]{1,2,0:T(8,128)S(1)} %copy.59, f32[1,8,512]{1,2,0:T(8,128)S(1)} %copy.58, f32[]{:T(128)} %constant.70.clone.2, pred[512]{0:T(512)(128)(4,1)S(1)} %compare_and_fusion, f32[8,16384]{0,1:T(8,128)} %bitcast.166, ...), kind=kCustom, calls=%fused_computation.21 | custom fusion | flops 16384 | bytes 1577480 | tf_op jit(solution)/shard_map/scatter-add | solution.py:134
  67.9 5.8 %copy.73 = f32[8,16,1024]{2,1,0:T(8,128)} copy(f32[8,16,1024]{0,2,1:T(8,128)} %bitcast.167) | data formatting | bytes 1048576 | tf_op jit(solution)/shard_map/reshape | solution.py:135
  73.7 1.4 pad_maximum_fusion
  77.3 2.9 reduce
  80.3 2.8 reshape.115
  83.1 3.9 copy.50
  87.0 11.9 %convolution_multiply_fusion.1 = f32[8,32,512]{2,1,0:T(8,128)S(1)} fusion(f32[8,32,512]{1,2,0:T(8,128)} %bitcast.176, f32[8,512,32]{1,2,0:T(8,128)S(1)} %copy-done.21), kind=kOutput, calls=%fused_computation.34 | convolution fusion | flops 809369600 | bytes 1572864 | tf_op jit(solution)/shard_map/lcy,yk->lck/dot_general | solution.py:82
  98.9 5.7 %fusion.48 = f32[8,32,512]{2,1,0:T(8,128)S(1)} fusion(f32[8,32,512]{2,1,0:T(8,128)S(1)} %convolution_multiply_fusion.1), kind=kOutput, calls=%fused_computation.49 | convolution fusion | flops 809238528 | bytes 1048576 | tf_op jit(solution)/shard_map/lck,ky->lcy/dot_general | solution.py:83
  104.5 2.0 copy.52
  106.5 3.3 reshape.116
  109.8 7.5 %all-to-all-start.1 = ((f32[32,1,4096]{2,1,0:T(1,128)}), f32[32,1,4096]{2,1,0:T(1,128)S(1)}, u32[]{:S(2)}, u32[]{:S(2)}) async-start(f32[32,1,4096]{2,1,0:T(1,128)} %reshape.116), calls=%async_computation.1 | async-start | bytes 1048576 | tf_op jit(solution)/shard_map/all_to_all | solution.py:84
  117.7 1.5 collective-permute-start.9
  120.7 3.5 collective-permute-start.1
  124.5 1.5 fusion.174
  128.4 1.6 collective-permute-done.2
  130.0 2.2 multiply_subtract_fusion.1
  134.0 6.0 %collective-permute-start.10 = (f32[8,1,1024]{2,1,0:T(1,128)S(1)}, f32[8,1,1024]{2,1,0:T(1,128)S(1)}, u32[]{:S(2)}, u32[]{:S(2)}) collective-permute-start(f32[8,1,1024]{2,1,0:T(1,128)S(1)} %get-tuple-element.64), channel_id=1, source_target_pairs={{1,0},{2,1},{3,2},{4,3},{5,4},{6,5},{7,6},{8,7},{9,8},{10,9},{11,1... | collective-permute-start | bytes 98312 | tf_op jit(solution)/shard_map/ppermute | solution.py:24
  140.0 2.7 collective-permute-start.5
  143.5 2.1 multiply_reduce_fusion.2
  145.6 2.8 reduce.1
  148.4 3.1 reshape.117
  151.5 4.2 copy.54
  155.7 3.1 all_to_all.59
  158.8 22.3 %multiply_reduce_fusion.3 = (f32[]{:T(128)}, f32[8,16,1024]{2,1,0:T(8,128)}) fusion(f32[8,20,1024]{2,1,0:T(8,128)} %get-tuple-element.22, f32[8,20,1024]{2,1,0:T(8,128)S(1)} %get-tuple-element.21, f32[8,16,1024]{2,1,0:T(8,128)S(1)} %multiply_subtract_fusion.1, f32[8,1,1024]{2,1,0:T(1,128)} %collective-permute-done.6, ...), kind=kOutput, calls=%fused_computation.143 | convolution fusion | flops 1629487104 | bytes 4784132 | tf_op jit(solution)/shard_map/lkr,kx->lrx/dot_general | solution.py:86
  181.0 82.0 %all-reduce.1 = (f32[]{:T(128)}, f32[]{:T(128)}) all-reduce(f32[]{:T(128)} %get-tuple-element.89, f32[]{:T(128)} %get-tuple-element.11), channel_id=1, replica_groups=mesh['tm'=8,'rows'=32] {'tm','rows'}, use_global_device_ids=true, to_apply=%region_2.3 | all-reduce | flops 2 | bytes 16 | tf_op jit(solution)/shard_map/psum | solution.py:130
  265.0 1.3 multiply_add_fusion.1
  266.2 19.9 %fusion.21 = f32[8,1024,16]{1,2,0:T(8,128)S(1)} fusion(f32[8,16,1024]{2,1,0:T(8,128)S(1)} %multiply_add_fusion.1), kind=kOutput, calls=%fused_computation.36 | convolution fusion | flops 1626341376 | bytes 1048576 | tf_op jit(solution)/shard_map/lrx,xk->lkr/dot_general | solution.py:80
  286.2 2.7 copy.62
  288.8 4.2 reshape.118
  293.0 5.2 %all-to-all-start.2 = ((f32[32,1,4096]{2,1,0:T(1,128)}), f32[32,1,4096]{2,1,0:T(1,128)}, u32[]{:S(2)}, u32[]{:S(2)}) async-start(f32[32,1,4096]{2,1,0:T(1,128)} %reshape.118), calls=%async_computation.2 | async-start | bytes 1048576 | tf_op jit(solution)/shard_map/all_to_all | solution.py:81
  298.3 1.3 collective-permute-start.17
  301.6 4.6 copy.75
  306.3 4.2 collective-permute-start.12
  310.5 9.6 %scatter_custom_fusion.1 = f32[8,16384]{0,1:T(8,128)} fusion(s32[512]{0:T(512)S(1)} %bitcast.183, f32[]{:T(128)} %constant.85.clone.1, f32[1,8,512]{1,2,0:T(8,128)} %copy-done.11, f32[1,8,512]{1,2,0:T(8,128)S(1)} %copy-done.10, f32[]{:T(128)} %constant.70.clone.2, pred[512]{0:T(512)(128)(4,1)S(1)} %compare_and_fusion, f32[8,16384]{0,1:T(8,128)} %bitcast.164, ...), kind=kCustom, calls=%fused_computation.19 | custom fusion | flops 16384 | bytes 1331720 | tf_op jit(solution)/shard_map/scatter-add | solution.py:134
  320.1 5.9 %copy.76 = f32[8,16,1024]{2,1,0:T(8,128)} copy(f32[8,16,1024]{0,2,1:T(8,128)} %bitcast.165) | data formatting | bytes 1048576 | tf_op jit(solution)/shard_map/reshape | solution.py:135
  326.0 3.7 reduce.2
  329.7 3.8 reshape.119
  333.5 3.8 copy.63
  337.3 12.0 %convolution_multiply_fusion = f32[8,32,512]{2,1,0:T(8,128)S(1)} fusion(f32[8,32,512]{1,2,0:T(8,128)} %bitcast.177, f32[8,512,32]{1,2,0:T(8,128)} %param.19), kind=kOutput, calls=%fused_computation.33 | convolution fusion | flops 809369600 | bytes 1572864 | tf_op jit(solution)/shard_map/lcy,yk->lck/dot_general | solution.py:82
  349.3 6.1 %fusion.45 = f32[8,32,512]{2,1,0:T(8,128)} fusion(f32[8,32,512]{2,1,0:T(8,128)S(1)} %convolution_multiply_fusion), kind=kOutput, calls=%fused_computation.46 | convolution fusion | flops 809238528 | bytes 1048576 | tf_op jit(solution)/shard_map/lck,ky->lcy/dot_general | solution.py:83
  355.4 3.0 copy.65
  358.5 3.1 reshape.120
  361.6 7.9 %all-to-all-start.3 = ((f32[32,1,4096]{2,1,0:T(1,128)}), f32[32,1,4096]{2,1,0:T(1,128)}, u32[]{:S(2)}, u32[]{:S(2)}) async-start(f32[32,1,4096]{2,1,0:T(1,128)} %reshape.120), calls=%async_computation.3 | async-start | bytes 1048576 | tf_op jit(solution)/shard_map/all_to_all | solution.py:84
  369.9 1.4 collective-permute-start.19
  371.8 3.5 collective-permute-start.13
  377.5 3.6 collective-permute-done.14
  382.8 6.0 %collective-permute-start.20 = (f32[8,1,1024]{2,1,0:T(1,128)S(1)}, f32[8,1,1024]{2,1,0:T(1,128)S(1)}, u32[]{:S(2)}, u32[]{:S(2)}) collective-permute-start(f32[8,1,1024]{2,1,0:T(1,128)S(1)} %get-tuple-element.32), channel_id=1, source_target_pairs={{1,0},{2,1},{3,2},{4,3},{5,4},{6,5},{7,6},{8,7},{9,8},{10,9},{11,1... | collective-permute-start | bytes 98312 | tf_op jit(solution)/shard_map/ppermute | solution.py:24
  389.6 1.4 collective-permute-start.16
  391.2 2.1 multiply_reduce_fusion
  393.3 3.7 reduce.3
  397.0 1.8 reshape.121
  398.8 2.6 copy.67
  401.4 2.4 all_to_all.67
  403.9 22.1 %multiply_reduce_fusion.1 = (f32[]{:T(128)}, f32[8,16,1024]{2,1,0:T(8,128)S(1)}) fusion(f32[8,20,1024]{2,1,0:T(8,128)} %get-tuple-element.22, f32[8,20,1024]{2,1,0:T(8,128)} %copy-done.5, f32[8,16,1024]{2,1,0:T(8,128)S(1)} %multiply_subtract_fusion, f32[8,1,1024]{2,1,0:T(1,128)S(1)} %collective-permute-done.16, ...), kind=kOutput, calls=%fused_computation.138 | convolution fusion | flops 1629487104 | bytes 4784132 | tf_op jit(solution)/shard_map/lkr,kx->lrx/dot_general | solution.py:86
  426.0 81.5 %all-reduce = (f32[]{:T(128)}, f32[]{:T(128)}) all-reduce(f32[]{:T(128)} %get-tuple-element.91, f32[]{:T(128)} %get-tuple-element.7), channel_id=1, replica_groups=mesh['tm'=8,'rows'=32] {'tm','rows'}, use_global_device_ids=true, to_apply=%region_7.9 | all-reduce | flops 2 | bytes 16 | tf_op jit(solution)/shard_map/psum | solution.py:130
  (132 shorter events, 21.4 us)
Async XLA Ops:
  4.9 68.8 %collective-permute-start.3 = (f32[2,8,2,2,1024]{4,3,1,2,0:T(2,128)}, f32[2,8,2,2,1024]{4,3,1,2,0:T(2,128)S(1)}, u32[]{:S(2)}, u32[]{:S(2)}) collective-permute-start(f32[2,8,2,2,1024]{4,3,1,2,0:T(2,128)} %get-tuple-element.17), channel_id=1, source_target_pairs={{0,1},{1,2},{2,3},{3,4},{4,5},{5,6},{6,7},{7,8},{8,9},{9,10},{10,1... | collective-permute-start | bytes 786440 | tf_op jit(solution)/shard_map/ppermute | solution.py:22
  7.6 66.1 %collective-permute-start.4 = (f32[2,8,2,2,1024]{4,3,1,2,0:T(2,128)}, f32[2,8,2,2,1024]{4,3,1,2,0:T(2,128)}, u32[]{:S(2)}, u32[]{:S(2)}) collective-permute-start(f32[2,8,2,2,1024]{4,3,1,2,0:T(2,128)} %get-tuple-element.18), channel_id=1, source_target_pairs={{1,0},{2,1},{3,2},{4,3},{5,4},{6,5},{7,6},{8,7},{9,8},{10,9},{11,1... | collective-permute-start | bytes 786440 | tf_op jit(solution)/shard_map/ppermute | solution.py:24
  8.2 109.2 %collective-permute-start.7 = (f32[8,16,1024]{2,1,0:T(8,128)}, f32[8,16,1024]{2,1,0:T(8,128)S(1)}, u32[]{:S(2)}, u32[]{:S(2)}) collective-permute-start(f32[8,16,1024]{2,1,0:T(8,128)} %bitcast.178), channel_id=1, source_target_pairs={{32,0},{64,32},{96,64},{128,96},{160,128},{192,160},{224,192},{33,... | collective-permute-start | bytes 1572872 | tf_op jit(solution)/shard_map/ppermute | solution.py:34
  9.5 110.1 %collective-permute-start = (f32[8,16,1024]{2,1,0:T(8,128)}, f32[8,16,1024]{2,1,0:T(8,128)}, u32[]{:S(2)}, u32[]{:S(2)}) collective-permute-start(f32[8,16,1024]{2,1,0:T(8,128)} %bitcast.179), channel_id=1, source_target_pairs={{0,32},{32,64},{64,96},{96,128},{128,160},{160,192},{192,224},{1,3... | collective-permute-start | bytes 1572872 | tf_op jit(solution)/shard_map/ppermute | solution.py:34
  35.6 18.2 %copy-start.18 = (s32[1,512]{1,0:T(1,128)S(1)}, s32[1,512]{1,0:T(1,128)}, u32[]{:S(2)}) copy-start(s32[1,512]{1,0:T(1,128)} %param.16) | copy-start | bytes 6148
  35.6 18.2 %copy-start.15 = (f32[1,8,16,1024]{3,2,1,0:T(8,128)S(1)}, f32[1,8,16,1024]{3,2,1,0:T(8,128)}, u32[]{:S(2)}) copy-start(f32[1,8,16,1024]{3,2,1,0:T(8,128)} %param.13) | copy-start | bytes 1572868
  43.4 33.2 %all-to-all-start = ((f32[32,1,4096]{2,1,0:T(1,128)}), f32[32,1,4096]{2,1,0:T(1,128)}, u32[]{:S(2)}, u32[]{:S(2)}) async-start(f32[32,1,4096]{2,1,0:T(1,128)} %reshape.114), calls=%async_computation | async-start | bytes 1048576 | tf_op jit(solution)/shard_map/all_to_all | solution.py:81
  53.9 4.7 copy-start.19
  53.9 4.8 copy-start.20
  58.7 9.2 %copy-start.9 = (f32[1,8,512]{1,2,0:T(8,128)}, f32[1,8,512]{1,2,0:T(8,128)S(1)}, u32[]{:S(2)}) copy-start(f32[1,8,512]{1,2,0:T(8,128)S(1)} %copy.58) | copy-start | bytes 49156
  58.8 9.1 %copy-start.11 = (f32[1,8,512]{1,2,0:T(8,128)}, f32[1,8,512]{1,2,0:T(8,128)S(1)}, u32[]{:S(2)}) copy-start(f32[1,8,512]{1,2,0:T(8,128)S(1)} %copy.59) | copy-start | bytes 49156
  76.7 82.1 %copy-start.5 = (f32[8,20,1024]{2,1,0:T(8,128)}, f32[8,20,1024]{2,1,0:T(8,128)S(1)}, u32[]{:S(2)}) copy-start(f32[8,20,1024]{2,1,0:T(8,128)S(1)} %get-tuple-element.21) | copy-start | bytes 1966084
  83.1 3.9 copy-start.21
  109.8 35.8 %all-to-all-start.1 = ((f32[32,1,4096]{2,1,0:T(1,128)}), f32[32,1,4096]{2,1,0:T(1,128)S(1)}, u32[]{:S(2)}, u32[]{:S(2)}) async-start(f32[32,1,4096]{2,1,0:T(1,128)} %reshape.116), calls=%async_computation.1 | async-start | bytes 1048576 | tf_op jit(solution)/shard_map/all_to_all | solution.py:84
  117.4 9.5 %collective-permute-start.8 = (f32[8,1,1024]{2,1,0:T(1,128)S(1)}, f32[8,1,1024]{2,1,0:T(1,128)S(1)}, u32[]{:S(2)}, u32[]{:S(2)}) collective-permute-start(f32[8,1,1024]{2,1,0:T(1,128)S(1)} %get-tuple-element.74), channel_id=1, source_target_pairs={{1,0},{2,1},{3,2},{4,3},{5,4},{6,5},{7,6},{8,7},{9,8},{10,9},{11,1... | collective-permute-start | bytes 98312 | tf_op jit(solution)/shard_map/ppermute | solution.py:24
  117.7 9.2 %collective-permute-start.9 = (f32[8,1,1024]{2,1,0:T(1,128)S(1)}, f32[8,1,1024]{2,1,0:T(1,128)S(1)}, u32[]{:S(2)}, u32[]{:S(2)}) collective-permute-start(f32[8,1,1024]{2,1,0:T(1,128)S(1)} %get-tuple-element.73), channel_id=1, source_target_pairs={{0,1},{1,2},{2,3},{3,4},{4,5},{5,6},{6,7},{7,8},{8,9},{9,10},{10,1... | collective-permute-start | bytes 98312 | tf_op jit(solution)/shard_map/ppermute | solution.py:22
  120.7 7.7 %collective-permute-start.1 = (f32[8,1,1024]{2,1,0:T(1,128)S(1)}, f32[8,1,1024]{2,1,0:T(1,128)S(1)}, u32[]{:S(2)}, u32[]{:S(2)}) collective-permute-start(f32[8,1,1024]{2,1,0:T(1,128)S(1)} %get-tuple-element.85), channel_id=1, source_target_pairs={{1,0},{2,1},{3,2},{4,3},{5,4},{6,5},{7,6},{8,7},{9,8},{10,9},{11,1... | collective-permute-start | bytes 98312 | tf_op jit(solution)/shard_map/ppermute | solution.py:24
  124.2 5.8 %collective-permute-start.2 = (f32[8,1,1024]{2,1,0:T(1,128)S(1)}, f32[8,1,1024]{2,1,0:T(1,128)S(1)}, u32[]{:S(2)}, u32[]{:S(2)}) collective-permute-start(f32[8,1,1024]{2,1,0:T(1,128)S(1)} %get-tuple-element.86), channel_id=1, source_target_pairs={{0,1},{1,2},{2,3},{3,4},{4,5},{5,6},{6,7},{7,8},{8,9},{9,10},{10,1... | collective-permute-start | bytes 98312 | tf_op jit(solution)/shard_map/ppermute | solution.py:22
  127.1 2.8 copy-start.7
  128.3 15.2 %copy-start.12 = (f32[8,16,1024]{2,1,0:T(8,128)S(1)}, f32[8,16,1024]{2,1,0:T(8,128)}, u32[]{:S(2)}) copy-start(f32[8,16,1024]{2,1,0:T(8,128)} %copy.73) | copy-start | bytes 1572868
  128.3 15.2 %copy-start.14 = (f32[1,8,16,1024]{3,2,1,0:T(8,128)S(1)}, f32[1,8,16,1024]{3,2,1,0:T(8,128)}, u32[]{:S(2)}) copy-start(f32[1,8,16,1024]{3,2,1,0:T(8,128)} %param.12) | copy-start | bytes 1572868
  134.0 8.9 %collective-permute-start.10 = (f32[8,1,1024]{2,1,0:T(1,128)S(1)}, f32[8,1,1024]{2,1,0:T(1,128)S(1)}, u32[]{:S(2)}, u32[]{:S(2)}) collective-permute-start(f32[8,1,1024]{2,1,0:T(1,128)S(1)} %get-tuple-element.64), channel_id=1, source_target_pairs={{1,0},{2,1},{3,2},{4,3},{5,4},{6,5},{7,6},{8,7},{9,8},{10,9},{11,1... | collective-permute-start | bytes 98312 | tf_op jit(solution)/shard_map/ppermute | solution.py:24
  139.9 3.3 collective-permute-start.11
  140.0 18.7 %collective-permute-start.5 = (f32[8,1,1024]{2,1,0:T(1,128)}, f32[8,1,1024]{2,1,0:T(1,128)}, u32[]{:S(2)}, u32[]{:S(2)}) collective-permute-start(f32[8,1,1024]{2,1,0:T(1,128)} %get-tuple-element.79), channel_id=1, source_target_pairs={{1,0},{2,1},{3,2},{4,3},{5,4},{6,5},{7,6},{8,7},{9,8},{10,9},{11,1... | collective-permute-start | bytes 98312 | tf_op jit(solution)/shard_map/ppermute | solution.py:24
  142.7 16.1 %collective-permute-start.6 = (f32[8,1,1024]{2,1,0:T(1,128)}, f32[8,1,1024]{2,1,0:T(1,128)}, u32[]{:S(2)}, u32[]{:S(2)}) collective-permute-start(f32[8,1,1024]{2,1,0:T(1,128)} %get-tuple-element.80), channel_id=1, source_target_pairs={{0,1},{1,2},{2,3},{3,4},{4,5},{5,6},{6,7},{7,8},{8,9},{9,10},{10,1... | collective-permute-start | bytes 98312 | tf_op jit(solution)/shard_map/ppermute | solution.py:22
  148.4 10.4 %copy-start.16 = (f32[1,8,16,1024]{3,2,1,0:T(8,128)S(1)}, f32[1,8,16,1024]{3,2,1,0:T(8,128)}, u32[]{:S(2)}) copy-start(f32[1,8,16,1024]{3,2,1,0:T(8,128)} %param.13) | copy-start | bytes 1572868
  266.2 32.0 %copy-start = (f32[8,16,1024]{2,1,0:T(8,128)}, f32[8,16,1024]{2,1,0:T(8,128)S(1)}, u32[]{:S(2)}) copy-start(f32[8,16,1024]{2,1,0:T(8,128)S(1)} %multiply_add_fusion.1) | copy-start | bytes 1572868
  293.0 32.9 %all-to-all-start.2 = ((f32[32,1,4096]{2,1,0:T(1,128)}), f32[32,1,4096]{2,1,0:T(1,128)}, u32[]{:S(2)}, u32[]{:S(2)}) async-start(f32[32,1,4096]{2,1,0:T(1,128)} %reshape.118), calls=%async_computation.2 | async-start | bytes 1048576 | tf_op jit(solution)/shard_map/all_to_all | solution.py:81
  298.3 71.2 %collective-permute-start.17 = (f32[8,16,1024]{2,1,0:T(8,128)S(1)}, f32[8,16,1024]{2,1,0:T(8,128)S(1)}, u32[]{:S(2)}, u32[]{:S(2)}) collective-permute-start(f32[8,16,1024]{2,1,0:T(8,128)S(1)} %multiply_add_fusion.1), channel_id=1, source_target_pairs={{32,0},{64,32},{96,64},{128,96},{160,128},{192,160},{224,192},{33,... | collective-permute-start | bytes 1572872 | tf_op jit(solution)/shard_map/ppermute | solution.py:34
  300.8 0.8 copy-start.3
  301.6 8.9 %copy-start.10 = (f32[1,8,512]{1,2,0:T(8,128)S(1)}, f32[1,8,512]{1,2,0:T(8,128)}, u32[]{:S(2)}) copy-start(f32[1,8,512]{1,2,0:T(8,128)} %copy-done.9) | copy-start | bytes 49156
  306.3 65.4 %collective-permute-start.12 = (f32[8,16,1024]{2,1,0:T(8,128)}, f32[8,16,1024]{2,1,0:T(8,128)S(1)}, u32[]{:S(2)}, u32[]{:S(2)}) collective-permute-start(f32[8,16,1024]{2,1,0:T(8,128)} %copy-done.3), channel_id=1, source_target_pairs={{0,32},{32,64},{64,96},{96,128},{128,160},{160,192},{192,224},{1,3... | collective-permute-start | bytes 1572872 | tf_op jit(solution)/shard_map/ppermute | solution.py:34
  361.6 31.7 %all-to-all-start.3 = ((f32[32,1,4096]{2,1,0:T(1,128)}), f32[32,1,4096]{2,1,0:T(1,128)}, u32[]{:S(2)}, u32[]{:S(2)}) async-start(f32[32,1,4096]{2,1,0:T(1,128)} %reshape.120), calls=%async_computation.3 | async-start | bytes 1048576 | tf_op jit(solution)/shard_map/all_to_all | solution.py:84
  369.5 6.4 %collective-permute-start.18 = (f32[8,1,1024]{2,1,0:T(1,128)S(1)}, f32[8,1,1024]{2,1,0:T(1,128)S(1)}, u32[]{:S(2)}, u32[]{:S(2)}) collective-permute-start(f32[8,1,1024]{2,1,0:T(1,128)S(1)} %get-tuple-element.42), channel_id=1, source_target_pairs={{1,0},{2,1},{3,2},{4,3},{5,4},{6,5},{7,6},{8,7},{9,8},{10,9},{11,1... | collective-permute-start | bytes 98312 | tf_op jit(solution)/shard_map/ppermute | solution.py:24
  369.9 6.0 %collective-permute-start.19 = (f32[8,1,1024]{2,1,0:T(1,128)S(1)}, f32[8,1,1024]{2,1,0:T(1,128)S(1)}, u32[]{:S(2)}, u32[]{:S(2)}) collective-permute-start(f32[8,1,1024]{2,1,0:T(1,128)S(1)} %get-tuple-element.41), channel_id=1, source_target_pairs={{0,1},{1,2},{2,3},{3,4},{4,5},{5,6},{6,7},{7,8},{8,9},{9,10},{10,1... | collective-permute-start | bytes 98312 | tf_op jit(solution)/shard_map/ppermute | solution.py:22
  371.8 5.7 %collective-permute-start.13 = (f32[8,1,1024]{2,1,0:T(1,128)S(1)}, f32[8,1,1024]{2,1,0:T(1,128)S(1)}, u32[]{:S(2)}, u32[]{:S(2)}) collective-permute-start(f32[8,1,1024]{2,1,0:T(1,128)S(1)} %get-tuple-element.53), channel_id=1, source_target_pairs={{1,0},{2,1},{3,2},{4,3},{5,4},{6,5},{7,6},{8,7},{9,8},{10,9},{11,1... | collective-permute-start | bytes 98312 | tf_op jit(solution)/shard_map/ppermute | solution.py:24
  375.3 5.8 %collective-permute-start.14 = (f32[8,1,1024]{2,1,0:T(1,128)S(1)}, f32[8,1,1024]{2,1,0:T(1,128)S(1)}, u32[]{:S(2)}, u32[]{:S(2)}) collective-permute-start(f32[8,1,1024]{2,1,0:T(1,128)S(1)} %get-tuple-element.54), channel_id=1, source_target_pairs={{0,1},{1,2},{2,3},{3,4},{4,5},{5,6},{6,7},{7,8},{8,9},{9,10},{10,1... | collective-permute-start | bytes 98312 | tf_op jit(solution)/shard_map/ppermute | solution.py:22
  376.1 5.0 copy-start.6
  376.1 5.0 copy-start.8
  377.3 13.8 %copy-start.1 = (f32[8,16,1024]{2,1,0:T(8,128)S(1)}, f32[8,16,1024]{2,1,0:T(8,128)}, u32[]{:S(2)}) copy-start(f32[8,16,1024]{2,1,0:T(8,128)} %copy-done) | copy-start | bytes 1572868
  377.4 13.8 %copy-start.13 = (f32[8,16,1024]{2,1,0:T(8,128)S(1)}, f32[8,16,1024]{2,1,0:T(8,128)}, u32[]{:S(2)}) copy-start(f32[8,16,1024]{2,1,0:T(8,128)} %copy.76) | copy-start | bytes 1572868
  382.8 8.1 %collective-permute-start.20 = (f32[8,1,1024]{2,1,0:T(1,128)S(1)}, f32[8,1,1024]{2,1,0:T(1,128)S(1)}, u32[]{:S(2)}, u32[]{:S(2)}) collective-permute-start(f32[8,1,1024]{2,1,0:T(1,128)S(1)} %get-tuple-element.32), channel_id=1, source_target_pairs={{1,0},{2,1},{3,2},{4,3},{5,4},{6,5},{7,6},{8,7},{9,8},{10,9},{11,1... | collective-permute-start | bytes 98312 | tf_op jit(solution)/shard_map/ppermute | solution.py:24
  388.9 2.1 collective-permute-start.21
  388.9 14.9 %collective-permute-start.15 = (f32[8,1,1024]{2,1,0:T(1,128)S(1)}, f32[8,1,1024]{2,1,0:T(1,128)S(1)}, u32[]{:S(2)}, u32[]{:S(2)}) collective-permute-start(f32[8,1,1024]{2,1,0:T(1,128)S(1)} %get-tuple-element.47), channel_id=1, source_target_pairs={{1,0},{2,1},{3,2},{4,3},{5,4},{6,5},{7,6},{8,7},{9,8},{10,9},{11,1... | collective-permute-start | bytes 98312 | tf_op jit(solution)/shard_map/ppermute | solution.py:24
  389.6 14.3 %collective-permute-start.16 = (f32[8,1,1024]{2,1,0:T(1,128)S(1)}, f32[8,1,1024]{2,1,0:T(1,128)S(1)}, u32[]{:S(2)}, u32[]{:S(2)}) collective-permute-start(f32[8,1,1024]{2,1,0:T(1,128)S(1)} %get-tuple-element.48), channel_id=1, source_target_pairs={{0,1},{1,2},{2,3},{3,4},{4,5},{5,6},{6,7},{7,8},{8,9},{9,10},{10,1... | collective-permute-start | bytes 98312 | tf_op jit(solution)/shard_map/ppermute | solution.py:22
  397.0 6.8 %copy-start.4 = (f32[8,16,1024]{2,1,0:T(8,128)S(1)}, f32[8,16,1024]{2,1,0:T(8,128)}, u32[]{:S(2)}) copy-start(f32[8,16,1024]{2,1,0:T(8,128)} %copy-done.3) | copy-start | bytes 1572868
  403.9 105.6 %copy-start.2 = (f32[8,16,1024]{2,1,0:T(8,128)S(1)}, f32[8,16,1024]{2,1,0:T(8,128)}, u32[]{:S(2)}) copy-start(f32[8,16,1024]{2,1,0:T(8,128)} %copy-done) | copy-start | bytes 1572868
  403.9 106.5 %copy-start.17 = (f32[8,16,1024]{2,1,0:T(8,128)S(1)}, f32[8,16,1024]{2,1,0:T(8,128)}, u32[]{:S(2)}) copy-start(f32[8,16,1024]{2,1,0:T(8,128)} %get-tuple-element.8) | copy-start | bytes 1572868
where the time goes:
time: 521 us; the launch traced here: 512 us
  blocking collectives  163 us (31%)
  matrix products  121 us (23%)
  local copies, waits for them, and re-layouts  92.9 us (18%)
  starting transfers between devices  73.4 us (14%)
  other arithmetic  49.2 us (9%)
  between operations  5.67 us (1%)
  waiting for transfers between devices  5.61 us (1%)
    psum x2, blocking collectives, on_device(): total_lam = lax.psum(jnp.sum(r_lam * r_lam), ('tm', 'rows'))  163 us
    dot_general x2, matrix products, covariance(): return jnp.einsum('lkr,kx->lrx', row_again, table_x, precision=HIGH) / whole  44.4 us
    dot_general x2, matrix products, covariance(): column_side = jnp.einsum('lrx,xk->lkr', field, table_x, precision=HIGH)  41.3 us
    unnamed x55, local copies, waits for them, and re-layouts  32.1 us
    dot_general x2, matrix products, covariance(): jnp.einsum('lcy,yk->lck', columns, table_y, precision=HIGH) * spectrum_cols  24 us
    ppermute x9, starting transfers between devices, with_halo(): lax.ppermute(head, axis, [((i + 1) % count, i) for i in range(count)])  23.6 us
    scatter-add x2, other arithmetic, on_device(): jnp.zeros((levels, rows_dev * width), jnp.float32).at[:, cells]  18.6 us
    all_to_all x2, starting transfers between devices, covariance(): lax.all_to_all(column_side, 'rows', split_axis=1, concat_axis=2, tiled=True)  15.6 us
  transfers between devices with their start and end apart: 26, of which 3 were waited for; matrix products, arithmetic and copies ran while one was open for 35% of the time, Pallas kernels for 0%

commit v1 on v0

v1 whole, which is shorter than its diff:
```python
import functools
import math

import jax
import jax.numpy as jnp
import numpy as np
from jax import lax
from jax.experimental import pallas as pl
from jax.experimental.pallas import tpu as pltpu
from jax.sharding import PartitionSpec as P

MESH = pl.DeviceIdType.MESH
F32 = jnp.float32
BF16 = jnp.bfloat16
NU = 0.12
MID = 1.0 - 4.0 * NU
LEV = 8
ROW = 16
COL = 32


def cas_pair(length):
    count = np.arange(length)
    angle = (count[:, None] * count[None, :] % length) * (2.0 * math.pi / length)
    table = (np.cos(angle) + np.sin(angle)).astype(np.float32)
    high = table.astype(jnp.bfloat16)
    low = (table - high.astype(np.float32)).astype(jnp.bfloat16)
    return high, low


def dot(a, b):
    return lax.dot_general(a, b, (((1,), (0,)), ((), ())), preferred_element_type=F32)


def dot_t(a, b):
    return lax.dot_general(a, b, (((1,), (1,)), ((), ())), preferred_element_type=F32)


def split(x):
    high = x.astype(BF16)
    return high, (x - high.astype(F32)).astype(BF16)


def swap_blocks(tiles):
    lane = lax.broadcasted_iota(jnp.int32, tiles[0].shape, 1)
    low = lane < 64
    even = (lane // 32) % 2 == 0
    t = list(tiles)
    for i, j in ((0, 2), (1, 3)):
        a, b = t[i], t[j]
        t[i] = jnp.where(low, a, pltpu.roll(b, 64, 1))
        t[j] = jnp.where(low, pltpu.roll(a, 64, 1), b)
    for i, j in ((0, 1), (2, 3)):
        a, b = t[i], t[j]
        t[i] = jnp.where(even, a, pltpu.roll(b, 32, 1))
        t[j] = jnp.where(even, pltpu.roll(a, 96, 1), b)
    return t


def forward_pass(src, dst, count, u, v, shift, width):
    @pl.loop(0, count)
    def _(j):
        x = src[j + 1]
        xs = src[j]
        xn = src[j + 2]
        e = pltpu.roll(x, width - 1, 1)
        w = pltpu.roll(x, 1, 1)
        k = j + shift
        dst[j] = MID * x + NU * ((e + w) + (xn + xs)) - (u[k] * (e - w) + v[k] * (xn - xs))


def adjoint_pass(src, dst, count, u, v, shift, width):
    @pl.loop(0, count)
    def _(j):
        x = src[j + 1]
        xs = src[j]
        xn = src[j + 2]
        k = j + shift
        t = NU * x
        ux = u[k] * x
        e = pltpu.roll(t + ux, width - 1, 1)
        w = pltpu.roll(t - ux, 1, 1)
        dst[j] = MID * x + (e + w) + ((NU * xn + v[k + 1] * xn) + (NU * xs - v[k - 1] * xs))


def kernel(
    rows_n,
    tm_n,
    misfit_h,
    mult_h,
    inc_h,
    obs_ref,
    weight_ref,
    cells_ref,
    wind_h,
    choice_ref,
    spec_h,
    txh_h,
    txl_h,
    tyh_h,
    tyl_h,
    mult_out,
    inc_out,
    misfit_v,
    mult_v,
    inc_v,
    wind_v,
    spec_v,
    txh,
    txl,
    tyh,
    tyl,
    pm,
    pi,
    pw,
    pd,
    pr,
    own_u,
    own_v,
    prev_u,
    prev_v,
    mid,
    q0,
    zsend,
    zrecv,
    asend,
    arecv,
    freq,
    pair,
    ypair,
    spec,
    smul,
    onehot,
    wpair,
    bfield,
    ffield,
    part,
    part2,
    zsum,
    rsum,
    in_sem,
    halo_s,
    halo_r,
    z_s,
    z_r,
    a_s,
    a_r,
    sum_s,
    sum_r,
    out_sem,
):
    width = 32 * rows_n
    tall = ROW * rows_n
    groups = width // 128
    tile = min(256, width)
    ytile = min(256, tall)
    me = lax.axis_index("rows")
    sec = lax.axis_index("tm")
    up = lax.rem(me + 1, rows_n)
    down = lax.rem(me + rows_n - 1, rows_n)
    after = lax.rem(sec + 1, tm_n)
    before = lax.rem(sec + tm_n - 1, tm_n)

    class Load:
        def __init__(self, n, src, dst, grouped):
            self.n, self.dst = n, dst
            if grouped:
                for g in range(groups):
                    lanes = src.at[:, 128 * g : 128 * g + 128]
                    pltpu.make_async_copy(lanes, dst.at[g], in_sem.at[n]).start()
            else:
                pltpu.make_async_copy(src, dst, in_sem.at[n]).start()

        def wait(self):
            pltpu.make_async_copy(self.dst, self.dst, in_sem.at[self.n]).wait()

    loads = [
        Load(n, *each)
        for n, each in enumerate(
            (
                (mult_h, mult_v, True),
                (wind_h, wind_v, True),
                (inc_h, inc_v, True),
                (txh_h, txh, False),
                (txl_h, txl, False),
                (misfit_h, misfit_v, True),
                (spec_h, spec_v, False),
                (tyh_h, tyh, False),
                (tyl_h, tyl, False),
            )
        )
    ]

    barrier = pltpu.get_barrier_semaphore()

    @pl.loop(1, rows_n)
    def _(s):
        pl.semaphore_signal(
            barrier, inc=1, device_id={"rows": lax.rem(me + s, rows_n)}, device_id_type=MESH
        )

    @pl.loop(1, tm_n)
    def _(s):
        pl.semaphore_signal(
            barrier, inc=1, device_id={"tm": lax.rem(sec + s, tm_n)}, device_id_type=MESH
        )

    def regroup(src, dst):
        @pl.loop(0, ROW)
        def _(r):
            for g in range(groups):
                dst[r + 2, :, 128 * g : 128 * g + 128] = src[g, pl.ds(r, LEV, stride=ROW), :]

    loads[0].wait()
    regroup(mult_v, pm)
    loads[1].wait()
    regroup(wind_v, pw)
    loads[2].wait()
    regroup(inc_v, pi)

    pl.semaphore_wait(barrier, rows_n - 1 + tm_n - 1)

    def halo(field, n):
        to_down = pltpu.make_async_remote_copy(
            src_ref=field.at[pl.ds(2, 2)],
            dst_ref=field.at[pl.ds(18, 2)],
            send_sem=halo_s.at[2 * n],
            recv_sem=halo_r.at[2 * n],
            device_id={"rows": down},
            device_id_type=MESH,
        )
        to_up = pltpu.make_async_remote_copy(
            src_ref=field.at[pl.ds(16, 2)],
            dst_ref=field.at[pl.ds(0, 2)],
            send_sem=halo_s.at[2 * n + 1],
            recv_sem=halo_r.at[2 * n + 1],
            device_id={"rows": up},
            device_id_type=MESH,
        )
        to_down.start()
        to_up.start()
        return to_down, to_up

    def shift(n, target):
        copy = pltpu.make_async_remote_copy(
            src_ref=zsend.at[n],
            dst_ref=zrecv.at[n],
            send_sem=z_s.at[n],
            recv_sem=z_r.at[n],
            device_id={"tm": target},
            device_id_type=MESH,
        )
        copy.start()
        return copy

    def exchange(n):
        pltpu.make_async_copy(asend.at[n, me], arecv.at[n, me], a_r.at[n]).start()

        @pl.loop(1, rows_n)
        def _(s):
            other = lax.rem(me + s, rows_n)
            pltpu.make_async_remote_copy(
                src_ref=asend.at[n, other],
                dst_ref=arecv.at[n, me],
                send_sem=a_s.at[n],
                recv_sem=a_r.at[n],
                device_id={"rows": other},
                device_id_type=MESH,
            ).start()

    def arrived(n):
        pltpu.make_async_copy(arecv.at[n], arecv.at[n], a_r.at[n]).wait()

    def sent(n):
        done = asend.at[n, pl.ds(0, rows_n - 1)]
        pltpu.make_async_copy(done, done, a_s.at[n]).wait()

    def load_pair(read):
        @pl.loop(0, 8)
        def _(i):
            x = read(i)
            high, low = split(x)
            pair[pl.ds(pl.multiple_of(16 * i, 16), 16), :] = high
            pair[pl.ds(pl.multiple_of(128 + 16 * i, 16), 16), :] = low

    def times_table(store):
        @pl.loop(0, width // tile)
        def _(n):
            cols = pl.ds(pl.multiple_of(n * tile, tile), tile)
            both = dot(pair[...], txh[:, cols])
            store(n, cols, both[:128] + both[128:] + dot(pair[pl.ds(0, 128), :], txl[:, cols]))

    def to_columns(n):
        def store(t, cols, value):
            for h in range(tile // 128):
                freq[t * (tile // 128) + h] = value[:, 128 * h : 128 * h + 128]

        times_table(store)

        @pl.loop(0, groups)
        def _(g):
            for h in range(2):
                tiles = [freq[g, pl.ds(4 * h + i, ROW, stride=LEV), :] for i in range(4)]
                for j, t in enumerate(swap_blocks(tiles)):
                    asend[n, 4 * g + j, :, 128 * h : 128 * h + 128] = t

        exchange(n)

    def from_columns(n, dst):
        arrived(n)

        @pl.loop(0, groups)
        def _(g):
            for h in range(2):
                tiles = [arecv[n, 4 * g + j, :, 128 * h : 128 * h + 128] for j in range(4)]
                for i, t in enumerate(swap_blocks(tiles)):
                    freq[g, pl.ds(4 * h + i, ROW, stride=LEV), :] = t

        for g in range(groups):
            high, low = split(freq[g])
            pair[pl.ds(0, 128), 128 * g : 128 * g + 128] = high
            pair[pl.ds(128, 128), 128 * g : 128 * g + 128] = low

        def store(t, cols, value):
            dst[:, cols] = value

        times_table(store)

    def y_pair(read):
        @pl.loop(0, tall // 64)
        def _(i):
            rows = pl.ds(pl.multiple_of(64 * i, 64), 64)
            high, low = split(read(i, rows))
            ypair[rows, 0:256] = high
            ypair[rows, 256:512] = low

    def y_times(store):
        @pl.loop(0, tall // ytile)
        def _(i):
            rows = pl.ds(pl.multiple_of(i * ytile, ytile), ytile)
            both = dot(tyh[rows, :], ypair[...])
            low = dot(tyl[rows, :], ypair[:, 0:256])
            store(i, rows, both[:, 0:256] + both[:, 256:512] + low)

    def y_load(n):
        def read(i, rows):
            return arecv[n, pl.ds(4 * i, 4)].reshape(64, 256)

        y_pair(read)

    def y_back(n):
        def store(i, rows, value):
            asend[n, pl.ds(i * (ytile // ROW), ytile // ROW)] = value.reshape(ytile // ROW, ROW, 256)

        y_times(store)
        exchange(n)

    halos_w = halo(pw, 0)
    halos_i = halo(pi, 1)
    halos_m = halo(pm, 2)

    def read_m(i):
        return pm[pl.ds(2 + 2 * i, 2)].reshape(16, width)

    load_pair(read_m)
    loads[3].wait()
    loads[4].wait()
    to_columns(0)

    level = lax.broadcasted_iota(jnp.int32, (LEV, 1), 0)

    def picks(section):
        column = jnp.zeros((LEV, 1), jnp.int32)
        for l in range(LEV):
            column = jnp.where(level == l, choice_ref[section, l], column)
        return [jnp.broadcast_to(column == n, (LEV, width)) for n in range(4)]

    for copy in halos_w:
        copy.wait_recv()

    @pl.loop(0, ROW + 4)
    def _(r):
        half = 0.5 * pw[r]
        for section, u_ref, v_ref in ((sec, own_u, own_v), (before, prev_u, prev_v)):
            chosen = picks(section)
            for comp, ref in ((0, u_ref), (1, v_ref)):
                value = jnp.zeros((LEV, width), F32)
                for n in range(4):
                    row = jnp.broadcast_to(half[2 * n + comp : 2 * n + comp + 1], (LEV, width))
                    value = jnp.where(chosen[n], row, value)
                ref[r] = value

    for copy in halos_i:
        copy.wait_recv()
    forward_pass(pi, mid, ROW + 2, own_u, own_v, 1, width)
    forward_pass(mid, zsend.at[0], ROW, own_u, own_v, 2, width)
    z0 = shift(0, after)
    for copy in halos_m:
        copy.wait_recv()
    adjoint_pass(pm, mid, ROW + 2, prev_u, prev_v, 1, width)
    adjoint_pass(mid, zsend.at[1], ROW, prev_u, prev_v, 2, width)
    z1 = shift(1, before)

    cells = cells_ref[...]
    n_obs = cells.shape[1]
    obs_row = cells // width
    obs_col = lax.rem(cells, width)

    @pl.loop(0, width // 128)
    def _(i):
        base = pl.multiple_of(128 * i, 128)
        at = lax.broadcasted_iota(jnp.int32, (128, n_obs), 0) + base
        onehot[pl.ds(base, 128), :] = jnp.where(at == obs_col, 1.0, 0.0).astype(BF16)

    def gather():
        both = dot(pair[...], onehot[...])
        picked = both[:128] + both[128:]
        total = jnp.zeros((LEV, n_obs), F32)
        for r in range(ROW):
            total = total + jnp.where(obs_row == r, picked[LEV * r : LEV * r + LEV], 0.0)
        return total

    def scatter(values, store):
        for r in range(0, ROW, 2):
            x = jnp.concatenate(
                [jnp.where(obs_row == r, values, 0.0), jnp.where(obs_row == r + 1, values, 0.0)], axis=0
            )
            high, low = split(x)
            wpair[pl.ds(LEV * r, 16), :] = high
            wpair[pl.ds(128 + LEV * r, 16), :] = low

        @pl.loop(0, width // tile)
        def _(n):
            cols = pl.ds(pl.multiple_of(n * tile, tile), tile)
            both = dot_t(wpair[...], onehot[cols, :])
            store(cols, (both[:128] + both[128:]).reshape(ROW, LEV, tile))

    def read_i(i):
        return pi[pl.ds(2 + 2 * i, 2)].reshape(16, width)

    load_pair(read_i)
    weighted = weight_ref[...] * (obs_ref[...] - gather())

    def store_d(cols, value):
        pd[pl.ds(2, ROW), :, cols] = value - pm[pl.ds(2, ROW), :, cols]

    scatter(weighted, store_d)

    loads[5].wait()

    @pl.loop(0, ROW)
    def _(r):
        for g in range(groups):
            lanes = slice(128 * g, 128 * g + 128)
            q0[r, :, lanes] = misfit_v[g, pl.ds(r, LEV, stride=ROW), :] - pi[r + 2, :, lanes]

    loads[6].wait()

    @pl.loop(0, tall // 64)
    def _(i):
        rows = pl.ds(pl.multiple_of(64 * i, 64), 64)
        for h in range(2):
            spec[rows, 128 * h : 128 * h + 128] = jnp.concatenate(
                [spec_v[4 * h + l, rows, :] for l in range(4)], axis=1
            )

    whole = 1.0 / (width * tall)

    loads[7].wait()
    loads[8].wait()
    arrived(0)
    y_load(0)

    def store_sm(i, rows, value):
        smul[rows, :] = spec[rows, :] * value

    y_times(store_sm)

    def read_sm(i, rows):
        return smul[rows, :] * whole

    y_pair(read_sm)
    y_back(1)

    keep_back = jnp.where(sec < tm_n - 1, 1.0, 0.0)
    keep_front = jnp.where(sec > 0, 1.0, 0.0)
    z1.wait_recv()

    @pl.loop(0, ROW)
    def _(r):
        pd[r + 2] = pd[r + 2] + keep_back * zrecv[1, r]

    halos_d = halo(pd, 3)

    z0.wait_recv()

    @pl.loop(0, ROW)
    def _(r):
        q0[r] = q0[r] + keep_front * zrecv[0, r]

    def read_q(i):
        return q0[pl.ds(2 * i, 2)].reshape(16, width)

    load_pair(read_q)
    to_columns(2)

    for copy in halos_d:
        copy.wait_recv()
    forward_pass(pd, mid, ROW + 2, own_u, own_v, 1, width)
    forward_pass(mid, zsend.at[2], ROW, own_u, own_v, 2, width)
    z2 = shift(2, after)

    def read_d(i):
        return pd[pl.ds(2 + 2 * i, 2)].reshape(16, width)

    load_pair(read_d)

    def store_f(cols, value):
        ffield[:, :, cols] = value

    scatter(weight_ref[...] * gather(), store_f)

    from_columns(1, bfield)

    @pl.loop(0, ROW)
    def _(r):
        pr[r + 2] = q0[r] - bfield[pl.ds(pl.multiple_of(LEV * r, LEV), LEV), :]

    halos_r = halo(pr, 4)

    arrived(2)
    y_load(2)

    def store_rm(i, rows, value):
        smul[rows, :] = spec[rows, :] * (value - smul[rows, :]) * whole

    y_times(store_rm)

    def read_rm(i, rows):
        return smul[rows, :]

    y_pair(read_rm)
    y_back(3)

    for copy in halos_r:
        copy.wait_recv()
    adjoint_pass(pr, mid, ROW + 2, prev_u, prev_v, 1, width)
    adjoint_pass(mid, zsend.at[3], ROW, prev_u, prev_v, 2, width)
    z3 = shift(3, before)

    from_columns(3, bfield)
    z2.wait_recv()
    z3.wait_recv()

    def fields(r):
        a = pr[r + 2]
        b = bfield[pl.ds(pl.multiple_of(LEV * r, LEV), LEV), :]
        d = pd[r + 2]
        e = keep_front * zrecv[2, r] - d
        f = ffield[r]
        k = keep_back * zrecv[3, r] - a
        return a, b, d, e, f, k

    def fold(x):
        total = x[:, 0:128]
        for g in range(1, groups):
            total = total + x[:, 128 * g : 128 * g + 128]
        return total

    def products(r, sums):
        a, b, d, e, f, k = fields(r)
        pairs = (a, a), (b, b), (e, e), (a, b), (a, e), (b, e), (d, d), (f, f), (k, k), (d, f), (d, k), (f, k)
        return tuple(s + fold(x * y) for s, (x, y) in zip(sums, pairs))

    sums = lax.fori_loop(0, ROW, products, (jnp.zeros((LEV, 128), F32),) * 12)
    for n in range(12):
        part[pl.ds(n, 1), :] = jnp.sum(sums[n], axis=0, keepdims=True)
    part[pl.ds(12, 4), :] = jnp.zeros((4, 128), F32)

    def everywhere(own, slots, axis, here, count, n):
        pltpu.make_async_copy(own, slots.at[here], sum_r.at[n]).start()

        @pl.loop(1, count)
        def _(s):
            pltpu.make_async_remote_copy(
                src_ref=own,
                dst_ref=slots.at[here],
                send_sem=sum_s.at[n],
                recv_sem=sum_r.at[n],
                device_id={axis: lax.rem(here + s, count)},
                device_id_type=MESH,
            ).start()

        pltpu.make_async_copy(slots, slots, sum_r.at[n]).wait()
        return jnp.sum(slots[...], axis=0)

    part2[...] = everywhere(part, zsum, "tm", sec, tm_n, 0)
    total = jnp.sum(everywhere(part2, rsum, "rows", me, rows_n, 1), axis=1, keepdims=True)
    aa, bb, ee, ab, ae, be, dd, ff, kk, df, dk, fk = (total[n : n + 1] for n in range(12))
    t0 = aa / (aa + dd + 1e-6)
    s0 = 1.0 - t0
    lam = aa + t0 * t0 * bb + s0 * s0 * ee + 2.0 * (s0 * ae - t0 * ab - t0 * s0 * be)
    dx = dd + s0 * s0 * ff + t0 * t0 * kk + 2.0 * (t0 * dk - s0 * df - t0 * s0 * fk)
    lam = jnp.maximum(lam, 0.0)
    dx = jnp.maximum(dx, 0.0)
    t1 = lam / (lam + dx + 1e-6)
    s1 = 1.0 - t1

    @pl.loop(0, ROW)
    def _(r):
        a, b, d, e, f, k = fields(r)
        x = pm[r + 2] + t0 * a + t1 * (a - t0 * b + s0 * e)
        y = pi[r + 2] + s0 * d + s1 * (d - s0 * f + t0 * k)
        for g in range(groups):
            lanes = slice(128 * g, 128 * g + 128)
            mult_v[g, pl.ds(r, LEV, stride=ROW), :] = x[:, lanes]
            inc_v[g, pl.ds(r, LEV, stride=ROW), :] = y[:, lanes]

    for n, (src, dst) in enumerate(((mult_v, mult_out), (inc_v, inc_out))):
        for g in range(groups):
            lanes = dst.at[:, 128 * g : 128 * g + 128]
            pltpu.make_async_copy(src.at[g], lanes, out_sem.at[n]).start()
    for n, dst in enumerate((mult_out, inc_out)):
        pltpu.make_async_copy(dst, dst, out_sem.at[n]).wait()

    for pairs in (halos_w, halos_i, halos_m, halos_d, halos_r, (z0, z1, z2, z3)):
        for copy in pairs:
            copy.wait_send()
    for n in range(4):
        sent(n)
    gone = zsum.at[pl.ds(0, tm_n - 1)]
    pltpu.make_async_copy(gone, gone, sum_s.at[0]).wait()
    gone = rsum.at[pl.ds(0, rows_n - 1)]
    pltpu.make_async_copy(gone, gone, sum_s.at[1]).wait()


def solution(mesh):
    rows_n = mesh.shape["rows"]
    tm_n = mesh.shape["tm"]
    width = COL * rows_n
    tall = ROW * rows_n
    x_tables = cas_pair(width)
    y_tables = cas_pair(tall)

    def on_device(misfit, mult, inc, obs, weights, cells, wind, choice, spectrum):
        n_obs = cells.shape[1]
        field = (LEV * ROW, width)
        padded = (ROW + 4, LEV, width)
        lanes = (width // 128, LEV * ROW, 128)
        vm = pltpu.VMEM
        dma = pltpu.SemaphoreType.DMA
        scratch = [
            vm(lanes, F32),
            vm(lanes, F32),
            vm(lanes, F32),
            vm(lanes, F32),
            vm((LEV, tall, COL), F32),
            vm((width, width), BF16),
            vm((width, width), BF16),
            vm((tall, tall), BF16),
            vm((tall, tall), BF16),
        ]
        scratch += [vm(padded, F32)] * 9
        scratch += [
            vm((ROW + 2, LEV, width), F32),
            vm((ROW, LEV, width), F32),
            vm((4, ROW, LEV, width), F32),
            vm((4, ROW, LEV, width), F32),
            vm((4, rows_n, ROW, LEV * COL), F32),
            vm((4, rows_n, ROW, LEV * COL), F32),
            vm((width // 128, 128, 128), F32),
            vm((256, width), BF16),
            vm((tall, 512), BF16),
            vm((tall, 256), F32),
            vm((tall, 256), F32),
            vm((width, n_obs), BF16),
            vm((256, n_obs), BF16),
            vm(field, F32),
            vm((ROW, LEV, width), F32),
            vm((16, 128), F32),
            vm((16, 128), F32),
            vm((tm_n, 16, 128), F32),
            vm((rows_n, 16, 128), F32),
            dma((9,)),
            dma((10,)),
            dma((10,)),
            dma((4,)),
            dma((4,)),
            dma((4,)),
            dma((4,)),
            dma((2,)),
            dma((2,)),
            dma((2,)),
        ]
        anywhere = pl.BlockSpec(memory_space=pl.ANY)
        near = pl.BlockSpec(memory_space=pltpu.VMEM)
        outs = pl.pallas_call(
            functools.partial(kernel, rows_n, tm_n),
            out_shape=(jax.ShapeDtypeStruct(field, F32),) * 2,
            in_specs=[
                anywhere,
                anywhere,
                anywhere,
                near,
                near,
                near,
                anywhere,
                pl.BlockSpec(memory_space=pltpu.SMEM),
                anywhere,
                anywhere,
                anywhere,
                anywhere,
                anywhere,
            ],
            out_specs=(anywhere, anywhere),
            scratch_shapes=scratch,
            compiler_params=pltpu.CompilerParams(
                collective_id=0, has_side_effects=True, vmem_limit_bytes=56 * 1024 * 1024
            ),
            name="saddle",
        )(
            misfit.reshape(field),
            mult.reshape(field),
            inc.reshape(field),
            obs[0],
            weights[0],
            cells,
            wind.reshape(field),
            choice,
            spectrum,
            *(jnp.asarray(t) for t in x_tables),
            *(jnp.asarray(t) for t in y_tables),
        )
        return tuple(o.reshape(1, LEV, ROW, width) for o in outs)

    return jax.shard_map(
        on_device,
        mesh=mesh,
        in_specs=(
            P("tm", None, "rows", None),
            P("tm", None, "rows", None),
            P("tm", None, "rows", None),
            P("tm", None, "rows"),
            P("tm", None, "rows"),
            P("tm", "rows"),
            P(None, None, "rows", None),
            P(),
            P(None, None, "rows"),
        ),
        out_specs=(P("tm", None, "rows", None), P("tm", None, "rows", None)),
        check_vma=False,
    )
```

time: 521 us -> 88.3 us (0.17); the launches traced: 512 us -> 88 us
  blocking collectives: 163 us -> 0 us
  matrix products: 121 us -> 0 us
  local copies, waits for them, and re-layouts: 92.9 us -> 6.77 us
  Pallas kernels: 0 us -> 80.6 us
  starting transfers between devices: 73.4 us -> 0 us
  other arithmetic: 49.2 us -> 0 us
  waiting for transfers between devices: 5.61 us -> 0 us
    psum x2 -> x0, blocking collectives: 163 us -> none  [on_device(): total_lam = lax.psum(jnp.sum(r_lam * r_lam), ('tm', 'rows'))]
    dot_general x8 -> x0, matrix products: 121 us -> none  [the longest x2 44.4 us: covariance(): return jnp.einsum('lkr,kx->lrx', row_again, table_x, precision=HIGH) / whole]
    pallas_call x0 -> x1, Pallas kernels: none -> 80.6 us  [on_device(): pl.pallas_call(functools.partial(kernel, rows_n, tm_n), out_shape=(jax.Sh...]
    ppermute x22 -> x0, starting transfers between devices: 42.4 us -> none  [the longest x9 23.6 us: with_halo(): lax.ppermute(head, axis, [((i + 1) % count, i) for i in range(count)])]
    all_to_all x4 -> x0, starting transfers between devices: 30.9 us -> none  [the longest x2 15.6 us: covariance(): lax.all_to_all(column_side, 'rows', split_axis=1, concat_axis=2, tiled=True)]
    unnamed x55 -> x3, local copies, waits for them, and re-layouts: 32.1 us -> 6.77 us
    all_to_all x7 -> x0, local copies, waits for them, and re-layouts: 20.6 us -> none  [the longest x4 12.2 us: covariance(): lax.all_to_all(returned, 'rows', split_axis=2, concat_axis=1, tiled=True)]
    scatter-add x2 -> x0, other arithmetic: 18.6 us -> none  [on_device(): jnp.zeros((levels, rows_dev * width), jnp.float32).at[:, cells]]
  transfers between devices with their start and end apart: 26 -> 0, of which waited for: 3 -> 0; matrix products, arithmetic and copies ran while one was open for 35% -> 0% of each run, Pallas kernels for 0% -> 0%
where the time goes in v1:
time: 88.3 us; the launch traced here: 88 us
  Pallas kernels  80.6 us (91%)
  local copies, waits for them, and re-layouts  6.77 us (8%)
    pallas_call x1, Pallas kernels, on_device(): pl.pallas_call(functools.partial(kernel, rows_n, tm_n), out_shape=(jax.Sh...  80.6 us
    unnamed x3, local copies, waits for them, and re-layouts  6.77 us

profile of v1, /device:TPU:1, one launch (start us, length us, event | category | flops | bytes accessed | tf_op | source)
XLA Modules:
  0.0 88.0 jit_solution(12811797561147477163)
XLA Ops:
  0.6 3.0 %copy.15.spec_h = f32[8,512,32]{2,1,0:T(8,128)} copy(f32[8,512,32]{1,2,0:T(8,128)} %param.21) | data formatting | bytes 1048576 | tf_op args[8]
  3.6 80.6 %saddle.1 = (f32[128,1024]{1,0:T(8,128)}, f32[128,1024]{1,0:T(8,128)}) custom-call(f32[128,1024]{1,0:T(8,128)} %bitcast.8, f32[128,1024]{1,0:T(8,128)} %bitcast.9, f32[128,1024]{1,0:T(8,128)} %bitcast.10, f32[8,512]{1,0:T(8,128)} %bitcast.14, f32[8,512]{1,0:T(8,128)} %bitcast.15, s32[1,512]{1,0:T(1,128)} %cells_ref.1, f32[128,1024]{1,0:T(8,128)} %bitcast.11, ...), custom_call_target="tpu_custom_call" | custom-call | tf_op jit(solution)/shard_map/saddle/pallas_call | solution.py:697
  84.3 1.9 %copy.18 = f32[1,8,16,1024]{3,2,1,0:T(8,128)} copy(f32[1,8,16,1024]{3,2,1,0:T(8,128)} %bitcast.13) | data formatting | bytes 1048576
  86.2 1.9 %copy.19 = f32[1,8,16,1024]{3,2,1,0:T(8,128)} copy(f32[1,8,16,1024]{3,2,1,0:T(8,128)} %bitcast.12) | data formatting | bytes 1048576

commit v2 on v1

--- a/solution.py
+++ b/solution.py
@@ -57,8 +57,8 @@
     return t
 
 
-def forward_pass(src, dst, count, u, v, shift, width):
-    @pl.loop(0, count)
+def forward_pass(src, store, first, last, u, v, shift, width):
+    @pl.loop(first, last, unroll=2)
     def _(j):
         x = src[j + 1]
         xs = src[j]
@@ -66,11 +66,11 @@
         e = pltpu.roll(x, width - 1, 1)
         w = pltpu.roll(x, 1, 1)
         k = j + shift
-        dst[j] = MID * x + NU * ((e + w) + (xn + xs)) - (u[k] * (e - w) + v[k] * (xn - xs))
-
-
-def adjoint_pass(src, dst, count, u, v, shift, width):
-    @pl.loop(0, count)
+        store(j, MID * x + NU * ((e + w) + (xn + xs)) - (u[k] * (e - w) + v[k] * (xn - xs)))
+
+
+def adjoint_pass(src, store, first, last, u, v, shift, width):
+    @pl.loop(first, last, unroll=2)
     def _(j):
         x = src[j + 1]
         xs = src[j]
@@ -80,7 +80,7 @@
         ux = u[k] * x
         e = pltpu.roll(t + ux, width - 1, 1)
         w = pltpu.roll(t - ux, 1, 1)
-        dst[j] = MID * x + (e + w) + ((NU * xn + v[k + 1] * xn) + (NU * xs - v[k - 1] * xs))
+        store(j, MID * x + (e + w) + ((NU * xn + v[k + 1] * xn) + (NU * xs - v[k - 1] * xs)))
 
 
 def kernel(
@@ -121,8 +121,12 @@
     prev_v,
     mid,
     q0,
-    zsend,
-    zrecv,
+    xi,
+    xm,
+    xd,
+    xr,
+    efield,
+    kfield,
     asend,
     arecv,
     freq,
@@ -161,6 +165,20 @@
     after = lax.rem(sec + 1, tm_n)
     before = lax.rem(sec + tm_n - 1, tm_n)
 
+    barrier = pltpu.get_barrier_semaphore()
+
+    @pl.loop(1, rows_n)
+    def _(s):
+        pl.semaphore_signal(
+            barrier, inc=1, device_id={"rows": lax.rem(me + s, rows_n)}, device_id_type=MESH
+        )
+
+    @pl.loop(1, tm_n)
+    def _(s):
+        pl.semaphore_signal(
+            barrier, inc=1, device_id={"tm": lax.rem(sec + s, tm_n)}, device_id_type=MESH
+        )
+
     class Load:
         def __init__(self, n, src, dst, grouped):
             self.n, self.dst = n, dst
@@ -179,10 +197,10 @@
         for n, each in enumerate(
             (
                 (mult_h, mult_v, True),
+                (txh_h, txh, False),
+                (txl_h, txl, False),
                 (wind_h, wind_v, True),
                 (inc_h, inc_v, True),
-                (txh_h, txh, False),
-                (txl_h, txl, False),
                 (misfit_h, misfit_v, True),
                 (spec_h, spec_v, False),
                 (tyh_h, tyh, False),
@@ -191,34 +209,11 @@
         )
     ]
 
-    barrier = pltpu.get_barrier_semaphore()
-
-    @pl.loop(1, rows_n)
-    def _(s):
-        pl.semaphore_signal(
-            barrier, inc=1, device_id={"rows": lax.rem(me + s, rows_n)}, device_id_type=MESH
-        )
-
-    @pl.loop(1, tm_n)
-    def _(s):
-        pl.semaphore_signal(
-            barrier, inc=1, device_id={"tm": lax.rem(sec + s, tm_n)}, device_id_type=MESH
-        )
-
-    def regroup(src, dst):
+    def regroup(src, dst, first):
         @pl.loop(0, ROW)
         def _(r):
             for g in range(groups):
-                dst[r + 2, :, 128 * g : 128 * g + 128] = src[g, pl.ds(r, LEV, stride=ROW), :]
-
-    loads[0].wait()
-    regroup(mult_v, pm)
-    loads[1].wait()
-    regroup(wind_v, pw)
-    loads[2].wait()
-    regroup(inc_v, pi)
-
-    pl.semaphore_wait(barrier, rows_n - 1 + tm_n - 1)
+                dst[r + first, :, 128 * g : 128 * g + 128] = src[g, pl.ds(r, LEV, stride=ROW), :]
 
     def halo(field, n):
         to_down = pltpu.make_async_remote_copy(
@@ -241,27 +236,48 @@
         to_up.start()
         return to_down, to_up
 
-    def shift(n, target):
-        copy = pltpu.make_async_remote_copy(
-            src_ref=zsend.at[n],
-            dst_ref=zrecv.at[n],
-            send_sem=z_s.at[n],
-            recv_sem=z_r.at[n],
-            device_id={"tm": target},
-            device_id_type=MESH,
-        )
-        copy.start()
-        return copy
-
-    def exchange(n):
-        pltpu.make_async_copy(asend.at[n, me], arecv.at[n, me], a_r.at[n]).start()
+    def shift(src, dst, n, target):
+        for first, count, sem in ((0, 2, 0), (14, 2, 0), (2, 8, 1), (10, 4, 2)):
+            pltpu.make_async_remote_copy(
+                src_ref=src.at[pl.ds(first, count)],
+                dst_ref=dst.at[pl.ds(2 + first, count)],
+                send_sem=z_s.at[n],
+                recv_sem=z_r.at[n, sem],
+                device_id={"tm": target},
+                device_id_type=MESH,
+            ).start()
+
+    def edges(dst, n):
+        rows = dst.at[pl.ds(0, 4)]
+        pltpu.make_async_copy(rows, rows, z_r.at[n, 0]).wait()
+        return halo(dst, n + 1)
+
+    def front(dst, n, halos):
+        rows = dst.at[pl.ds(4, 8)]
+        pltpu.make_async_copy(rows, rows, z_r.at[n, 1]).wait()
+        for copy in halos:
+            copy.wait_recv()
+
+    def back(dst, n):
+        rows = dst.at[pl.ds(12, 4)]
+        pltpu.make_async_copy(rows, rows, z_r.at[n, 2]).wait()
+
+    def twice(one_pass, src, store, u, v, half):
+        def store_mid(j, value):
+            mid[j] = value
+
+        one_pass(src, store_mid, 10 * half, 10 + 8 * half, u, v, 1, width)
+        one_pass(mid, store, 8 * half, 8 + 8 * half, u, v, 2, width)
+
+    def exchange(n, rows=slice(None)):
+        pltpu.make_async_copy(asend.at[n, me, rows], arecv.at[n, me, rows], a_r.at[n]).start()
 
         @pl.loop(1, rows_n)
         def _(s):
             other = lax.rem(me + s, rows_n)
             pltpu.make_async_remote_copy(
-                src_ref=asend.at[n, other],
-                dst_ref=arecv.at[n, me],
+                src_ref=asend.at[n, other, rows],
+                dst_ref=arecv.at[n, me, rows],
                 send_sem=a_s.at[n],
                 recv_sem=a_r.at[n],
                 device_id={"rows": other},
@@ -304,7 +320,29 @@
                 for j, t in enumerate(swap_blocks(tiles)):
                     asend[n, 4 * g + j, :, 128 * h : 128 * h + 128] = t
 
-        exchange(n)
+    def half_to_columns(n, read, half):
+        @pl.loop(0, 4)
+        def _(i):
+            high, low = split(read(4 * half + i))
+            pair[pl.ds(pl.multiple_of(128 * half + 16 * i, 16), 16), :] = high
+            pair[pl.ds(pl.multiple_of(128 * half + 64 + 16 * i, 16), 16), :] = low
+
+        @pl.loop(0, width // tile)
+        def _(t):
+            cols = pl.ds(pl.multiple_of(t * tile, tile), tile)
+            both = dot(pair[pl.ds(128 * half, 128), :], txh[:, cols])
+            value = both[:64] + both[64:] + dot(pair[pl.ds(128 * half, 64), :], txl[:, cols])
+            for h in range(tile // 128):
+                freq[t * (tile // 128) + h, pl.ds(64 * half, 64)] = value[:, 128 * h : 128 * h + 128]
+
+        @pl.loop(0, groups)
+        def _(g):
+            for h in range(2):
+                tiles = [freq[g, pl.ds(64 * half + 4 * h + i, 8, stride=LEV), :] for i in range(4)]
+                for j, t in enumerate(swap_blocks(tiles)):
+                    asend[n, 4 * g + j, 8 * half : 8 * half + 8, 128 * h : 128 * h + 128] = t
+
+        exchange(n, pl.ds(8 * half, 8))
 
     def from_columns(n, dst):
         arrived(n)
@@ -355,17 +393,89 @@
         y_times(store)
         exchange(n)
 
+    def read_m(i):
+        return pm[pl.ds(2 * i, 2)].reshape(16, width)
+
+    loads[0].wait()
+    regroup(mult_v, pm, 0)
+    load_pair(read_m)
+    loads[1].wait()
+    loads[2].wait()
+    to_columns(0)
+    loads[3].wait()
+    regroup(wind_v, pw, 2)
+    loads[4].wait()
+    regroup(inc_v, pi, 0)
+
+    pl.semaphore_wait(barrier, rows_n - 1 + tm_n - 1)
     halos_w = halo(pw, 0)
-    halos_i = halo(pi, 1)
-    halos_m = halo(pm, 2)
-
-    def read_m(i):
-        return pm[pl.ds(2 + 2 * i, 2)].reshape(16, width)
-
-    load_pair(read_m)
-    loads[3].wait()
-    loads[4].wait()
-    to_columns(0)
+    exchange(0)
+    shift(pi, xi, 0, after)
+    shift(pm, xm, 1, before)
+
+    cells = cells_ref[...]
+    n_obs = cells.shape[1]
+    obs_row = cells // width
+    obs_col = lax.rem(cells, width)
+
+    @pl.loop(0, width // 128)
+    def _(i):
+        base = pl.multiple_of(128 * i, 128)
+        at = lax.broadcasted_iota(jnp.int32, (128, n_obs), 0) + base
+        onehot[pl.ds(base, 128), :] = jnp.where(at == obs_col, 1.0, 0.0).astype(BF16)
+
+    def gather():
+        both = dot(pair[...], onehot[...])
+        picked = both[:128] + both[128:]
+        total = jnp.zeros((LEV, n_obs), F32)
+        for r in range(ROW):
+            total = total + jnp.where(obs_row == r, picked[LEV * r : LEV * r + LEV], 0.0)
+        return total
+
+    def scatter(values, store):
+        for r in range(0, ROW, 2):
+            x = jnp.concatenate(
+                [jnp.where(obs_row == r, values, 0.0), jnp.where(obs_row == r + 1, values, 0.0)], axis=0
+            )
+            high, low = split(x)
+            wpair[pl.ds(LEV * r, 16), :] = high
+            wpair[pl.ds(128 + LEV * r, 16), :] = low
+
+        @pl.loop(0, width // tile)
+        def _(n):
+            cols = pl.ds(pl.multiple_of(n * tile, tile), tile)
+            both = dot_t(wpair[...], onehot[cols, :])
+            store(cols, (both[:128] + both[128:]).reshape(ROW, LEV, tile))
+
+    def read_i(i):
+        return pi[pl.ds(2 * i, 2)].reshape(16, width)
+
+    load_pair(read_i)
+    weighted = weight_ref[...] * (obs_ref[...] - gather())
+
+    def store_d(cols, value):
+        pd[:, :, cols] = value - pm[:, :, cols]
+
+    scatter(weighted, store_d)
+
+    loads[5].wait()
+
+    @pl.loop(0, ROW)
+    def _(r):
+        for g in range(groups):
+            lanes = slice(128 * g, 128 * g + 128)
+            q0[r, :, lanes] = misfit_v[g, pl.ds(r, LEV, stride=ROW), :] - pi[r, :, lanes]
+
+    loads[6].wait()
+
+    @pl.loop(0, tall // 128)
+    def _(i):
+        rows = pl.ds(pl.multiple_of(128 * i, 128), 128)
+        for h in range(2):
+            lanes = slice(128 * h, 128 * h + 128)
+            spec[rows, lanes] = spec_v[lanes, rows].T
+
+    whole = 1.0 / (width * tall)
 
     level = lax.broadcasted_iota(jnp.int32, (LEV, 1), 0)
 
@@ -390,81 +500,8 @@
                     value = jnp.where(chosen[n], row, value)
                 ref[r] = value
 
-    for copy in halos_i:
-        copy.wait_recv()
-    forward_pass(pi, mid, ROW + 2, own_u, own_v, 1, width)
-    forward_pass(mid, zsend.at[0], ROW, own_u, own_v, 2, width)
-    z0 = shift(0, after)
-    for copy in halos_m:
-        copy.wait_recv()
-    adjoint_pass(pm, mid, ROW + 2, prev_u, prev_v, 1, width)
-    adjoint_pass(mid, zsend.at[1], ROW, prev_u, prev_v, 2, width)
-    z1 = shift(1, before)
-
-    cells = cells_ref[...]
-    n_obs = cells.shape[1]
-    obs_row = cells // width
-    obs_col = lax.rem(cells, width)
-
-    @pl.loop(0, width // 128)
-    def _(i):
-        base = pl.multiple_of(128 * i, 128)
-        at = lax.broadcasted_iota(jnp.int32, (128, n_obs), 0) + base
-        onehot[pl.ds(base, 128), :] = jnp.where(at == obs_col, 1.0, 0.0).astype(BF16)
-
-    def gather():
-        both = dot(pair[...], onehot[...])
-        picked = both[:128] + both[128:]
-        total = jnp.zeros((LEV, n_obs), F32)
-        for r in range(ROW):
-            total = total + jnp.where(obs_row == r, picked[LEV * r : LEV * r + LEV], 0.0)
-        return total
-
-    def scatter(values, store):
-        for r in range(0, ROW, 2):
-            x = jnp.concatenate(
-                [jnp.where(obs_row == r, values, 0.0), jnp.where(obs_row == r + 1, values, 0.0)], axis=0
-            )
-            high, low = split(x)
-            wpair[pl.ds(LEV * r, 16), :] = high
-            wpair[pl.ds(128 + LEV * r, 16), :] = low
-
-        @pl.loop(0, width // tile)
-        def _(n):
-            cols = pl.ds(pl.multiple_of(n * tile, tile), tile)
-            both = dot_t(wpair[...], onehot[cols, :])
-            store(cols, (both[:128] + both[128:]).reshape(ROW, LEV, tile))
-
-    def read_i(i):
-        return pi[pl.ds(2 + 2 * i, 2)].reshape(16, width)
-
-    load_pair(read_i)
-    weighted = weight_ref[...] * (obs_ref[...] - gather())
-
-    def store_d(cols, value):
-        pd[pl.ds(2, ROW), :, cols] = value - pm[pl.ds(2, ROW), :, cols]
-
-    scatter(weighted, store_d)
-
-    loads[5].wait()
-
-    @pl.loop(0, ROW)
-    def _(r):
-        for g in range(groups):
-            lanes = slice(128 * g, 128 * g + 128)
-            q0[r, :, lanes] = misfit_v[g, pl.ds(r, LEV, stride=ROW), :] - pi[r + 2, :, lanes]
-
-    loads[6].wait()
-
-    @pl.loop(0, tall // 64)
-    def _(i):
-        rows = pl.ds(pl.multiple_of(64 * i, 64), 64)
-        for h in range(2):
-            spec[rows, 128 * h : 128 * h + 128] = jnp.concatenate(
-                [spec_v[4 * h + l, rows, :] for l in range(4)], axis=1
-            )
-
-    whole = 1.0 / (width * tall)
+    halos_i = edges(xi, 0)
+    halos_m = edges(xm, 1)
 
     loads[7].wait()
     loads[8].wait()
@@ -484,34 +521,39 @@
 
     keep_back = jnp.where(sec < tm_n - 1, 1.0, 0.0)
     keep_front = jnp.where(sec > 0, 1.0, 0.0)
-    z1.wait_recv()
+
+    def store_q(j, value):
+        q0[j] = q0[j] + keep_front * value
+
+    def read_q(i):
+        return q0[pl.ds(2 * i, 2)].reshape(16, width)
+
+    front(xi, 0, halos_i)
+    twice(forward_pass, xi, store_q, prev_u, prev_v, 0)
+    half_to_columns(2, read_q, 0)
+    back(xi, 0)
+    twice(forward_pass, xi, store_q, prev_u, prev_v, 1)
+    half_to_columns(2, read_q, 1)
+
+    def store_back(j, value):
+        pd[j] = pd[j] + keep_back * value
+
+    front(xm, 1, halos_m)
+    twice(adjoint_pass, xm, store_back, own_u, own_v, 0)
+    back(xm, 1)
+    twice(adjoint_pass, xm, store_back, own_u, own_v, 1)
+    shift(pd, xd, 2, after)
+
+    from_columns(1, bfield)
 
     @pl.loop(0, ROW)
     def _(r):
-        pd[r + 2] = pd[r + 2] + keep_back * zrecv[1, r]
-
-    halos_d = halo(pd, 3)
-
-    z0.wait_recv()
-
-    @pl.loop(0, ROW)
-    def _(r):
-        q0[r] = q0[r] + keep_front * zrecv[0, r]
-
-    def read_q(i):
-        return q0[pl.ds(2 * i, 2)].reshape(16, width)
-
-    load_pair(read_q)
-    to_columns(2)
-
-    for copy in halos_d:
-        copy.wait_recv()
-    forward_pass(pd, mid, ROW + 2, own_u, own_v, 1, width)
-    forward_pass(mid, zsend.at[2], ROW, own_u, own_v, 2, width)
-    z2 = shift(2, after)
+        pr[r] = q0[r] - bfield[pl.ds(pl.multiple_of(LEV * r, LEV), LEV), :]
+
+    shift(pr, xr, 3, before)
 
     def read_d(i):
-        return pd[pl.ds(2 + 2 * i, 2)].reshape(16, width)
+        return pd[pl.ds(2 * i, 2)].reshape(16, width)
 
     load_pair(read_d)
 
@@ -520,13 +562,7 @@
 
     scatter(weight_ref[...] * gather(), store_f)
 
-    from_columns(1, bfield)
-
-    @pl.loop(0, ROW)
-    def _(r):
-        pr[r + 2] = q0[r] - bfield[pl.ds(pl.multiple_of(LEV * r, LEV), LEV), :]
-
-    halos_r = halo(pr, 4)
+    halos_d = edges(xd, 2)
 
     arrived(2)
     y_load(2)
@@ -542,24 +578,22 @@
     y_pair(read_rm)
     y_back(3)
 
-    for copy in halos_r:
-        copy.wait_recv()
-    adjoint_pass(pr, mid, ROW + 2, prev_u, prev_v, 1, width)
-    adjoint_pass(mid, zsend.at[3], ROW, prev_u, prev_v, 2, width)
-    z3 = shift(3, before)
-
-    from_columns(3, bfield)
-    z2.wait_recv()
-    z3.wait_recv()
-
-    def fields(r):
-        a = pr[r + 2]
-        b = bfield[pl.ds(pl.multiple_of(LEV * r, LEV), LEV), :]
-        d = pd[r + 2]
-        e = keep_front * zrecv[2, r] - d
-        f = ffield[r]
-        k = keep_back * zrecv[3, r] - a
-        return a, b, d, e, f, k
+    halos_r = edges(xr, 3)
+
+    def store_e(j, value):
+        efield[j] = keep_front * value - pd[j]
+
+    def store_k(j, value):
+        kfield[j] = keep_back * value - pr[j]
+
+    front(xd, 2, halos_d)
+    twice(forward_pass, xd, store_e, prev_u, prev_v, 0)
+    back(xd, 2)
+    twice(forward_pass, xd, store_e, prev_u, prev_v, 1)
+    front(xr, 3, halos_r)
+    twice(adjoint_pass, xr, store_k, own_u, own_v, 0)
+    back(xr, 3)
+    twice(adjoint_pass, xr, store_k, own_u, own_v, 1)
 
     def fold(x):
         total = x[:, 0:128]
@@ -567,15 +601,34 @@
             total = total + x[:, 128 * g : 128 * g + 128]
         return total
 
-    def products(r, sums):
-        a, b, d, e, f, k = fields(r)
-        pairs = (a, a), (b, b), (e, e), (a, b), (a, e), (b, e), (d, d), (f, f), (k, k), (d, f), (d, k), (f, k)
-        return tuple(s + fold(x * y) for s, (x, y) in zip(sums, pairs))
-
-    sums = lax.fori_loop(0, ROW, products, (jnp.zeros((LEV, 128), F32),) * 12)
-    for n in range(12):
-        part[pl.ds(n, 1), :] = jnp.sum(sums[n], axis=0, keepdims=True)
-    part[pl.ds(12, 4), :] = jnp.zeros((4, 128), F32)
+    def inner(count, pairs_of):
+        def step(r, sums):
+            return tuple(s + fold(x * y) for s, (x, y) in zip(sums, pairs_of(r)))
+
+        return lax.fori_loop(0, ROW, step, (jnp.zeros((LEV, 128), F32),) * count)
+
+    def pairs_early(r):
+        a, d, e, f, k = pr[r], pd[r], efield[r], ffield[r], kfield[r]
+        return (a, a), (e, e), (a, e), (d, d), (f, f), (k, k), (d, f), (d, k), (f, k)
+
+    early = inner(9, pairs_early)
+
+    from_columns(3, bfield)
+
+    def filtered(r):
+        return bfield[pl.ds(pl.multiple_of(LEV * r, LEV), LEV), :]
+
+    def pairs_late(r):
+        b = filtered(r)
+        return (b, b), (pr[r], b), (b, efield[r])
+
+    late = inner(3, pairs_late)
+    lane = lax.broadcasted_iota(jnp.int32, (1, 128), 1)
+    row = jnp.zeros((1, 128), F32)
+    for n, value in enumerate(early + late):
+        one = jnp.sum(jnp.sum(value, axis=0, keepdims=True), axis=1, keepdims=True)
+        row = jnp.where(lane == n, one, row)
+    part[...] = row
 
     def everywhere(own, slots, axis, here, count, n):
         pltpu.make_async_copy(own, slots.at[here], sum_r.at[n]).start()
@@ -595,8 +648,8 @@
         return jnp.sum(slots[...], axis=0)
 
     part2[...] = everywhere(part, zsum, "tm", sec, tm_n, 0)
-    total = jnp.sum(everywhere(part2, rsum, "rows", me, rows_n, 1), axis=1, keepdims=True)
-    aa, bb, ee, ab, ae, be, dd, ff, kk, df, dk, fk = (total[n : n + 1] for n in range(12))
+    total = everywhere(part2, rsum, "rows", me, rows_n, 1)
+    aa, ee, ae, dd, ff, kk, df, dk, fk, bb, ab, be = (total[:, n : n + 1] for n in range(12))
     t0 = aa / (aa + dd + 1e-6)
     s0 = 1.0 - t0
     lam = aa + t0 * t0 * bb + s0 * s0 * ee + 2.0 * (s0 * ae - t0 * ab - t0 * s0 * be)
@@ -608,9 +661,9 @@
 
     @pl.loop(0, ROW)
     def _(r):
-        a, b, d, e, f, k = fields(r)
-        x = pm[r + 2] + t0 * a + t1 * (a - t0 * b + s0 * e)
-        y = pi[r + 2] + s0 * d + s1 * (d - s0 * f + t0 * k)
+        a, b, d, e, f, k = pr[r], filtered(r), pd[r], efield[r], ffield[r], kfield[r]
+        x = pm[r] + t0 * a + t1 * (a - t0 * b + s0 * e)
+        y = pi[r] + s0 * d + s1 * (d - s0 * f + t0 * k)
         for g in range(groups):
             lanes = slice(128 * g, 128 * g + 128)
             mult_v[g, pl.ds(r, LEV, stride=ROW), :] = x[:, lanes]
@@ -623,9 +676,11 @@
     for n, dst in enumerate((mult_out, inc_out)):
         pltpu.make_async_copy(dst, dst, out_sem.at[n]).wait()
 
-    for pairs in (halos_w, halos_i, halos_m, halos_d, halos_r, (z0, z1, z2, z3)):
-        for copy in pairs:
+    for copies in (halos_w, halos_i, halos_m, halos_d, halos_r):
+        for copy in copies:
             copy.wait_send()
+    for n, src in enumerate((pi, pm, pd, pr)):
+        pltpu.make_async_copy(src, src, z_s.at[n]).wait()
     for n in range(4):
         sent(n)
     gone = zsum.at[pl.ds(0, tm_n - 1)]
@@ -654,18 +709,21 @@
             vm(lanes, F32),
             vm(lanes, F32),
             vm(lanes, F32),
-            vm((LEV, tall, COL), F32),
+            vm((LEV * COL, tall), F32),
             vm((width, width), BF16),
             vm((width, width), BF16),
             vm((tall, tall), BF16),
             vm((tall, tall), BF16),
         ]
-        scratch += [vm(padded, F32)] * 9
+        inner = (ROW, LEV, width)
+        scratch += [vm(inner, F32)] * 2 + [vm(padded, F32)] + [vm(inner, F32)] * 2
+        scratch += [vm(padded, F32)] * 4
         scratch += [
             vm((ROW + 2, LEV, width), F32),
-            vm((ROW, LEV, width), F32),
-            vm((4, ROW, LEV, width), F32),
-            vm((4, ROW, LEV, width), F32),
+            vm(inner, F32),
+        ]
+        scratch += [vm(padded, F32)] * 4 + [vm(inner, F32)] * 2
+        scratch += [
             vm((4, rows_n, ROW, LEV * COL), F32),
             vm((4, rows_n, ROW, LEV * COL), F32),
             vm((width // 128, 128, 128), F32),
@@ -677,15 +735,15 @@
             vm((256, n_obs), BF16),
             vm(field, F32),
             vm((ROW, LEV, width), F32),
-            vm((16, 128), F32),
-            vm((16, 128), F32),
-            vm((tm_n, 16, 128), F32),
-            vm((rows_n, 16, 128), F32),
+            vm((1, 128), F32),
+            vm((1, 128), F32),
+            vm((tm_n, 1, 128), F32),
+            vm((rows_n, 1, 128), F32),
             dma((9,)),
             dma((10,)),
             dma((10,)),
             dma((4,)),
-            dma((4,)),
+            dma((4, 3)),
             dma((4,)),
             dma((4,)),
             dma((2,)),
@@ -696,7 +754,7 @@
         near = pl.BlockSpec(memory_space=pltpu.VMEM)
         outs = pl.pallas_call(
             functools.partial(kernel, rows_n, tm_n),
-            out_shape=(jax.ShapeDtypeStruct(field, F32),) * 2,
+            out_shape=(pltpu.VMEM(field, F32),) * 2,
             in_specs=[
                 anywhere,
                 anywhere,
@@ -712,7 +770,7 @@
                 anywhere,
                 anywhere,
             ],
-            out_specs=(anywhere, anywhere),
+            out_specs=(near, near),
             scratch_shapes=scratch,
             compiler_params=pltpu.CompilerParams(
                 collective_id=0, has_side_effects=True, vmem_limit_bytes=56 * 1024 * 1024
@@ -727,7 +785,7 @@
             cells,
             wind.reshape(field),
             choice,
-            spectrum,
+            jnp.transpose(spectrum, (0, 2, 1)).reshape(LEV * COL, tall),
             *(jnp.asarray(t) for t in x_tables),
             *(jnp.asarray(t) for t in y_tables),
         )

time: 88.3 us -> 71.1 us (0.81)
  Pallas kernels: 80.6 us -> 68.6 us
  local copies, waits for them, and re-layouts: 6.77 us -> 1.59 us
    pallas_call x1, Pallas kernels: 80.6 us -> 68.6 us  [on_device(): pl.pallas_call(functools.partial(kernel, rows_n, tm_n), out_shape=(pltpu....]
    unnamed x3 -> x2, local copies, waits for them, and re-layouts: 6.77 us -> 1.59 us
where the time goes in v2:
time: 71.1 us; the launch traced here: 70.9 us
  Pallas kernels  68.6 us (96%)
  local copies, waits for them, and re-layouts  1.59 us (2%)
    pallas_call x1, Pallas kernels, on_device(): pl.pallas_call(functools.partial(kernel, rows_n, tm_n), out_shape=(pltpu....  68.6 us
    unnamed x2, local copies, waits for them, and re-layouts  1.59 us

profile of v2, /device:TPU:1, one launch (start us, length us, event | category | flops | bytes accessed | tf_op | source)
XLA Modules:
  0.0 70.9 jit_solution(14351900201041895650)
XLA Ops:
  0.6 68.6 %saddle.1 = (f32[128,1024]{1,0:T(8,128)S(1)}, f32[128,1024]{1,0:T(8,128)S(1)}) custom-call(f32[128,1024]{1,0:T(8,128)} %bitcast.13, f32[128,1024]{1,0:T(8,128)} %bitcast.14, f32[128,1024]{1,0:T(8,128)} %bitcast.15, f32[8,512]{1,0:T(8,128)} %bitcast.18, f32[8,512]{1,0:T(8,128)} %bitcast.19, s32[1,512]{1,0:T(1,128)} %cells_ref.1, f32[128,1024]{1,0:T(8,128)} %bitcast.16, ...), custom_call_target="tpu_custom_call" | custom-call | tf_op jit(solution)/shard_map/saddle/pallas_call | solution.py:755
  69.3 0.8 %copy.17 = f32[1,8,16,1024]{3,2,1,0:T(8,128)} copy(f32[1,8,16,1024]{3,2,1,0:T(8,128)S(1)} %bitcast.12) | data formatting | bytes 1048576
  70.1 0.8 %copy.18 = f32[1,8,16,1024]{3,2,1,0:T(8,128)} copy(f32[1,8,16,1024]{3,2,1,0:T(8,128)S(1)} %bitcast.11) | data formatting | bytes 1048576

commit v3 on v2

--- a/solution.py
+++ b/solution.py
@@ -58,7 +58,7 @@
 
 
 def forward_pass(src, store, first, last, u, v, shift, width):
-    @pl.loop(first, last, unroll=2)
+    @pl.loop(first, last, unroll=4)
     def _(j):
         x = src[j + 1]
         xs = src[j]
@@ -70,7 +70,7 @@
 
 
 def adjoint_pass(src, store, first, last, u, v, shift, width):
-    @pl.loop(first, last, unroll=2)
+    @pl.loop(first, last, unroll=4)
     def _(j):
         x = src[j + 1]
         xs = src[j]
@@ -210,7 +210,7 @@
     ]
 
     def regroup(src, dst, first):
-        @pl.loop(0, ROW)
+        @pl.loop(0, ROW, unroll=4)
         def _(r):
             for g in range(groups):
                 dst[r + first, :, 128 * g : 128 * g + 128] = src[g, pl.ds(r, LEV, stride=ROW), :]
@@ -269,30 +269,33 @@
         one_pass(src, store_mid, 10 * half, 10 + 8 * half, u, v, 1, width)
         one_pass(mid, store, 8 * half, 8 + 8 * half, u, v, 2, width)
 
-    def exchange(n, rows=slice(None)):
-        pltpu.make_async_copy(asend.at[n, me, rows], arecv.at[n, me, rows], a_r.at[n]).start()
+    def exchange(n, rows=slice(None), lanes=slice(None), sem=0):
+        pltpu.make_async_copy(
+            asend.at[n, me, rows, lanes], arecv.at[n, me, rows, lanes], a_r.at[n, sem]
+        ).start()
 
         @pl.loop(1, rows_n)
         def _(s):
             other = lax.rem(me + s, rows_n)
             pltpu.make_async_remote_copy(
-                src_ref=asend.at[n, other, rows],
-                dst_ref=arecv.at[n, me, rows],
+                src_ref=asend.at[n, other, rows, lanes],
+                dst_ref=arecv.at[n, me, rows, lanes],
                 send_sem=a_s.at[n],
-                recv_sem=a_r.at[n],
+                recv_sem=a_r.at[n, sem],
                 device_id={"rows": other},
                 device_id_type=MESH,
             ).start()
 
-    def arrived(n):
-        pltpu.make_async_copy(arecv.at[n], arecv.at[n], a_r.at[n]).wait()
+    def arrived(n, lanes=slice(None), sem=0):
+        blocks = arecv.at[n, :, :, lanes]
+        pltpu.make_async_copy(blocks, blocks, a_r.at[n, sem]).wait()
 
     def sent(n):
         done = asend.at[n, pl.ds(0, rows_n - 1)]
         pltpu.make_async_copy(done, done, a_s.at[n]).wait()
 
     def load_pair(read):
-        @pl.loop(0, 8)
+        @pl.loop(0, 8, unroll=4)
         def _(i):
             x = read(i)
             high, low = split(x)
@@ -300,7 +303,7 @@
             pair[pl.ds(pl.multiple_of(128 + 16 * i, 16), 16), :] = low
 
     def times_table(store):
-        @pl.loop(0, width // tile)
+        @pl.loop(0, width // tile, unroll=2)
         def _(n):
             cols = pl.ds(pl.multiple_of(n * tile, tile), tile)
             both = dot(pair[...], txh[:, cols])
@@ -313,7 +316,7 @@
 
         times_table(store)
 
-        @pl.loop(0, groups)
+        @pl.loop(0, groups, unroll=4)
         def _(g):
             for h in range(2):
                 tiles = [freq[g, pl.ds(4 * h + i, ROW, stride=LEV), :] for i in range(4)]
@@ -321,13 +324,13 @@
                     asend[n, 4 * g + j, :, 128 * h : 128 * h + 128] = t
 
     def half_to_columns(n, read, half):
-        @pl.loop(0, 4)
+        @pl.loop(0, 4, unroll=4)
         def _(i):
             high, low = split(read(4 * half + i))
             pair[pl.ds(pl.multiple_of(128 * half + 16 * i, 16), 16), :] = high
             pair[pl.ds(pl.multiple_of(128 * half + 64 + 16 * i, 16), 16), :] = low
 
-        @pl.loop(0, width // tile)
+        @pl.loop(0, width // tile, unroll=2)
         def _(t):
             cols = pl.ds(pl.multiple_of(t * tile, tile), tile)
             both = dot(pair[pl.ds(128 * half, 128), :], txh[:, cols])
@@ -335,7 +338,7 @@
             for h in range(tile // 128):
                 freq[t * (tile // 128) + h, pl.ds(64 * half, 64)] = value[:, 128 * h : 128 * h + 128]
 
-        @pl.loop(0, groups)
+        @pl.loop(0, groups, unroll=4)
         def _(g):
             for h in range(2):
                 tiles = [freq[g, pl.ds(64 * half + 4 * h + i, 8, stride=LEV), :] for i in range(4)]
@@ -345,12 +348,13 @@
         exchange(n, pl.ds(8 * half, 8))
 
     def from_columns(n, dst):
-        arrived(n)
-
-        @pl.loop(0, groups)
-        def _(g):
-            for h in range(2):
-                tiles = [arecv[n, 4 * g + j, :, 128 * h : 128 * h + 128] for j in range(4)]
+        for h in range(2):
+            lanes = pl.ds(128 * h, 128)
+            arrived(n, lanes, h)
+
+            @pl.loop(0, groups, unroll=4)
+            def _(g):
+                tiles = [arecv[n, 4 * g + j, :, lanes] for j in range(4)]
                 for i, t in enumerate(swap_blocks(tiles)):
                     freq[g, pl.ds(4 * h + i, ROW, stride=LEV), :] = t
 
@@ -364,34 +368,37 @@
 
         times_table(store)
 
-    def y_pair(read):
-        @pl.loop(0, tall // 64)
+    def y_pair(h, read):
+        @pl.loop(0, tall // 64, unroll=4)
         def _(i):
             rows = pl.ds(pl.multiple_of(64 * i, 64), 64)
-            high, low = split(read(i, rows))
-            ypair[rows, 0:256] = high
-            ypair[rows, 256:512] = low
-
-    def y_times(store):
-        @pl.loop(0, tall // ytile)
+            high, low = split(read(i, rows, pl.ds(128 * h, 128)))
+            ypair[rows, 256 * h : 256 * h + 128] = high
+            ypair[rows, 256 * h + 128 : 256 * h + 256] = low
+
+    def y_times(h, store):
+        @pl.loop(0, tall // ytile, unroll=2)
         def _(i):
             rows = pl.ds(pl.multiple_of(i * ytile, ytile), ytile)
-            both = dot(tyh[rows, :], ypair[...])
-            low = dot(tyl[rows, :], ypair[:, 0:256])
-            store(i, rows, both[:, 0:256] + both[:, 256:512] + low)
-
-    def y_load(n):
-        def read(i, rows):
-            return arecv[n, pl.ds(4 * i, 4)].reshape(64, 256)
-
-        y_pair(read)
-
-    def y_back(n):
-        def store(i, rows, value):
-            asend[n, pl.ds(i * (ytile // ROW), ytile // ROW)] = value.reshape(ytile // ROW, ROW, 256)
-
-        y_times(store)
-        exchange(n)
+            both = dot(tyh[rows, :], ypair[:, 256 * h : 256 * h + 256])
+            low = dot(tyl[rows, :], ypair[:, 256 * h : 256 * h + 128])
+            store(i, rows, pl.ds(128 * h, 128), both[:, 0:128] + both[:, 128:256] + low)
+
+    def filter_rows(came, goes, store, read):
+        def read_came(i, rows, lanes):
+            return arecv[came, pl.ds(4 * i, 4), :, lanes].reshape(64, 128)
+
+        def store_back(i, rows, lanes, value):
+            count = ytile // ROW
+            asend[goes, pl.ds(i * count, count), :, lanes] = value.reshape(count, ROW, 128)
+
+        arrived(came)
+        for h in range(2):
+            y_pair(h, read_came)
+            y_times(h, store)
+            y_pair(h, read)
+            y_times(h, store_back)
+            exchange(goes, slice(None), pl.ds(128 * h, 128), h)
 
     def read_m(i):
         return pm[pl.ds(2 * i, 2)].reshape(16, width)
@@ -418,7 +425,7 @@
     obs_row = cells // width
     obs_col = lax.rem(cells, width)
 
-    @pl.loop(0, width // 128)
+    @pl.loop(0, width // 128, unroll=2)
     def _(i):
         base = pl.multiple_of(128 * i, 128)
         at = lax.broadcasted_iota(jnp.int32, (128, n_obs), 0) + base
@@ -441,7 +448,7 @@
             wpair[pl.ds(LEV * r, 16), :] = high
             wpair[pl.ds(128 + LEV * r, 16), :] = low
 
-        @pl.loop(0, width // tile)
+        @pl.loop(0, width // tile, unroll=2)
         def _(n):
             cols = pl.ds(pl.multiple_of(n * tile, tile), tile)
             both = dot_t(wpair[...], onehot[cols, :])
@@ -460,7 +467,7 @@
 
     loads[5].wait()
 
-    @pl.loop(0, ROW)
+    @pl.loop(0, ROW, unroll=4)
     def _(r):
         for g in range(groups):
             lanes = slice(128 * g, 128 * g + 128)
@@ -468,7 +475,7 @@
 
     loads[6].wait()
 
-    @pl.loop(0, tall // 128)
+    @pl.loop(0, tall // 128, unroll=2)
     def _(i):
         rows = pl.ds(pl.multiple_of(128 * i, 128), 128)
         for h in range(2):
@@ -488,7 +495,7 @@
     for copy in halos_w:
         copy.wait_recv()
 
-    @pl.loop(0, ROW + 4)
+    @pl.loop(0, ROW + 4, unroll=2)
     def _(r):
         half = 0.5 * pw[r]
         for section, u_ref, v_ref in ((sec, own_u, own_v), (before, prev_u, prev_v)):
@@ -505,19 +512,14 @@
 
     loads[7].wait()
     loads[8].wait()
-    arrived(0)
-    y_load(0)
-
-    def store_sm(i, rows, value):
-        smul[rows, :] = spec[rows, :] * value
-
-    y_times(store_sm)
-
-    def read_sm(i, rows):
-        return smul[rows, :] * whole
-
-    y_pair(read_sm)
-    y_back(1)
+
+    def store_sm(i, rows, lanes, value):
+        smul[rows, lanes] = spec[rows, lanes] * value
+
+    def read_sm(i, rows, lanes):
+        return smul[rows, lanes] * whole
+
+    filter_rows(0, 1, store_sm, read_sm)
 
     keep_back = jnp.where(sec < tm_n - 1, 1.0, 0.0)
     keep_front = jnp.where(sec > 0, 1.0, 0.0)
@@ -546,7 +548,7 @@
 
     from_columns(1, bfield)
 
-    @pl.loop(0, ROW)
+    @pl.loop(0, ROW, unroll=4)
     def _(r):
         pr[r] = q0[r] - bfield[pl.ds(pl.multiple_of(LEV * r, LEV), LEV), :]
 
@@ -564,19 +566,13 @@
 
     halos_d = edges(xd, 2)
 
-    arrived(2)
-    y_load(2)
-
-    def store_rm(i, rows, value):
-        smul[rows, :] = spec[rows, :] * (value - smul[rows, :]) * whole
-
-    y_times(store_rm)
-
-    def read_rm(i, rows):
-        return smul[rows, :]
-
-    y_pair(read_rm)
-    y_back(3)
+    def store_rm(i, rows, lanes, value):
+        smul[rows, lanes] = spec[rows, lanes] * (value - smul[rows, lanes]) * whole
+
+    def read_rm(i, rows, lanes):
+        return smul[rows, lanes]
+
+    filter_rows(2, 3, store_rm, read_rm)
 
     halos_r = edges(xr, 3)
 
@@ -659,7 +655,7 @@
     t1 = lam / (lam + dx + 1e-6)
     s1 = 1.0 - t1
 
-    @pl.loop(0, ROW)
+    @pl.loop(0, ROW, unroll=4)
     def _(r):
         a, b, d, e, f, k = pr[r], filtered(r), pd[r], efield[r], ffield[r], kfield[r]
         x = pm[r] + t0 * a + t1 * (a - t0 * b + s0 * e)
@@ -745,7 +741,7 @@
             dma((4,)),
             dma((4, 3)),
             dma((4,)),
-            dma((4,)),
+            dma((4, 2)),
             dma((2,)),
             dma((2,)),
             dma((2,)),

time: 71.1 us -> 65.9 us (0.927)
  Pallas kernels: 68.6 us -> 63.5 us
    pallas_call x1, Pallas kernels: 68.6 us -> 63.5 us  [on_device(): pl.pallas_call(functools.partial(kernel, rows_n, tm_n), out_shape=(pltpu....]
where the time goes in v3:
time: 65.9 us; the launch traced here: 65.7 us
  Pallas kernels  63.5 us (96%)
  local copies, waits for them, and re-layouts  1.59 us (2%)
    pallas_call x1, Pallas kernels, on_device(): pl.pallas_call(functools.partial(kernel, rows_n, tm_n), out_shape=(pltpu....  63.5 us
    unnamed x2, local copies, waits for them, and re-layouts  1.59 us

profile of v3, /device:TPU:1, one launch (start us, length us, event | category | flops | bytes accessed | tf_op | source)
XLA Modules:
  0.0 65.7 jit_solution(4322730235103681455)
XLA Ops:
  0.6 63.5 %saddle.1 = (f32[128,1024]{1,0:T(8,128)S(1)}, f32[128,1024]{1,0:T(8,128)S(1)}) custom-call(f32[128,1024]{1,0:T(8,128)} %bitcast.13, f32[128,1024]{1,0:T(8,128)} %bitcast.14, f32[128,1024]{1,0:T(8,128)} %bitcast.15, f32[8,512]{1,0:T(8,128)} %bitcast.18, f32[8,512]{1,0:T(8,128)} %bitcast.19, s32[1,512]{1,0:T(1,128)} %cells_ref.1, f32[128,1024]{1,0:T(8,128)} %bitcast.16, ...), custom_call_target="tpu_custom_call" | custom-call | tf_op jit(solution)/shard_map/saddle/pallas_call | solution.py:751
  64.1 0.8 %copy.17 = f32[1,8,16,1024]{3,2,1,0:T(8,128)} copy(f32[1,8,16,1024]{3,2,1,0:T(8,128)S(1)} %bitcast.12) | data formatting | bytes 1048576
  64.9 0.8 %copy.18 = f32[1,8,16,1024]{3,2,1,0:T(8,128)} copy(f32[1,8,16,1024]{3,2,1,0:T(8,128)S(1)} %bitcast.11) | data formatting | bytes 1048576

commit v4 on v3

--- a/solution.py
+++ b/solution.py
@@ -151,7 +151,6 @@
     a_r,
     sum_s,
     sum_r,
-    out_sem,
 ):
     width = 32 * rows_n
     tall = ROW * rows_n
@@ -418,7 +417,6 @@
     halos_w = halo(pw, 0)
     exchange(0)
     shift(pi, xi, 0, after)
-    shift(pm, xm, 1, before)
 
     cells = cells_ref[...]
     n_obs = cells.shape[1]
@@ -464,6 +462,7 @@
         pd[:, :, cols] = value - pm[:, :, cols]
 
     scatter(weighted, store_d)
+    shift(pm, xm, 1, before)
 
     loads[5].wait()
 
@@ -588,6 +587,7 @@
     twice(forward_pass, xd, store_e, prev_u, prev_v, 1)
     front(xr, 3, halos_r)
     twice(adjoint_pass, xr, store_k, own_u, own_v, 0)
+    from_columns(3, bfield)
     back(xr, 3)
     twice(adjoint_pass, xr, store_k, own_u, own_v, 1)
 
@@ -608,8 +608,6 @@
         return (a, a), (e, e), (a, e), (d, d), (f, f), (k, k), (d, f), (d, k), (f, k)
 
     early = inner(9, pairs_early)
-
-    from_columns(3, bfield)
 
     def filtered(r):
         return bfield[pl.ds(pl.multiple_of(LEV * r, LEV), LEV), :]
@@ -665,12 +663,10 @@
             mult_v[g, pl.ds(r, LEV, stride=ROW), :] = x[:, lanes]
             inc_v[g, pl.ds(r, LEV, stride=ROW), :] = y[:, lanes]
 
-    for n, (src, dst) in enumerate(((mult_v, mult_out), (inc_v, inc_out))):
-        for g in range(groups):
-            lanes = dst.at[:, 128 * g : 128 * g + 128]
-            pltpu.make_async_copy(src.at[g], lanes, out_sem.at[n]).start()
-    for n, dst in enumerate((mult_out, inc_out)):
-        pltpu.make_async_copy(dst, dst, out_sem.at[n]).wait()
+    for g in range(groups):
+        lanes = slice(128 * g, 128 * g + 128)
+        mult_out[:, lanes] = mult_v[g]
+        inc_out[:, lanes] = inc_v[g]
 
     for copies in (halos_w, halos_i, halos_m, halos_d, halos_r):
         for copy in copies:
@@ -744,7 +740,6 @@
             dma((4, 2)),
             dma((2,)),
             dma((2,)),
-            dma((2,)),
         ]
         anywhere = pl.BlockSpec(memory_space=pl.ANY)
         near = pl.BlockSpec(memory_space=pltpu.VMEM)

time: 65.9 us -> 65.6 us (level)
  no operation moved by 1% of the time
where the time goes in v4:
time: 65.6 us; the launch traced here: 65.4 us
  Pallas kernels  63.1 us (96%)
  local copies, waits for them, and re-layouts  1.59 us (2%)
    pallas_call x1, Pallas kernels, on_device(): pl.pallas_call(functools.partial(kernel, rows_n, tm_n), out_shape=(pltpu....  63.1 us
    unnamed x2, local copies, waits for them, and re-layouts  1.59 us

profile of v4, /device:TPU:1, one launch (start us, length us, event | category | flops | bytes accessed | tf_op | source)
XLA Modules:
  0.0 65.4 jit_solution(8159938091776556146)
XLA Ops:
  0.6 63.1 %saddle.1 = (f32[128,1024]{1,0:T(8,128)S(1)}, f32[128,1024]{1,0:T(8,128)S(1)}) custom-call(f32[128,1024]{1,0:T(8,128)} %bitcast.13, f32[128,1024]{1,0:T(8,128)} %bitcast.14, f32[128,1024]{1,0:T(8,128)} %bitcast.15, f32[8,512]{1,0:T(8,128)} %bitcast.18, f32[8,512]{1,0:T(8,128)} %bitcast.19, s32[1,512]{1,0:T(1,128)} %cells_ref.1, f32[128,1024]{1,0:T(8,128)} %bitcast.16, ...), custom_call_target="tpu_custom_call" | custom-call | tf_op jit(solution)/shard_map/saddle/pallas_call | solution.py:746
  63.8 0.8 %copy.17 = f32[1,8,16,1024]{3,2,1,0:T(8,128)} copy(f32[1,8,16,1024]{3,2,1,0:T(8,128)S(1)} %bitcast.12) | data formatting | bytes 1048576
  64.6 0.8 %copy.18 = f32[1,8,16,1024]{3,2,1,0:T(8,128)} copy(f32[1,8,16,1024]{3,2,1,0:T(8,128)S(1)} %bitcast.11) | data formatting | bytes 1048576

commit v5 on v4

--- a/solution.py
+++ b/solution.py
@@ -166,16 +166,16 @@
 
     barrier = pltpu.get_barrier_semaphore()
 
+    @pl.loop(1, tm_n)
+    def _(s):
+        pl.semaphore_signal(
+            barrier, inc=1, device_id={"tm": lax.rem(sec + s, tm_n)}, device_id_type=MESH
+        )
+
     @pl.loop(1, rows_n)
     def _(s):
         pl.semaphore_signal(
             barrier, inc=1, device_id={"rows": lax.rem(me + s, rows_n)}, device_id_type=MESH
-        )
-
-    @pl.loop(1, tm_n)
-    def _(s):
-        pl.semaphore_signal(
-            barrier, inc=1, device_id={"tm": lax.rem(sec + s, tm_n)}, device_id_type=MESH
         )
 
     class Load:
@@ -601,7 +601,7 @@
         def step(r, sums):
             return tuple(s + fold(x * y) for s, (x, y) in zip(sums, pairs_of(r)))
 
-        return lax.fori_loop(0, ROW, step, (jnp.zeros((LEV, 128), F32),) * count)
+        return lax.fori_loop(0, ROW, step, (jnp.zeros((LEV, 128), F32),) * count, unroll=2)
 
     def pairs_early(r):
         a, d, e, f, k = pr[r], pd[r], efield[r], ffield[r], kfield[r]

time: 65.6 us -> 65.4 us (level)
  no operation moved by 1% of the time
where the time goes in v5:
time: 65.4 us; the launch traced here: 65.2 us
  Pallas kernels  63 us (96%)
  local copies, waits for them, and re-layouts  1.59 us (2%)
    pallas_call x1, Pallas kernels, on_device(): pl.pallas_call(functools.partial(kernel, rows_n, tm_n), out_shape=(pltpu....  63 us
    unnamed x2, local copies, waits for them, and re-layouts  1.59 us

profile of v5, /device:TPU:1, one launch (start us, length us, event | category | flops | bytes accessed | tf_op | source)
XLA Modules:
  0.0 65.2 jit_solution(16934732539374265033)
XLA Ops:
  0.6 63.0 %saddle.1 = (f32[128,1024]{1,0:T(8,128)S(1)}, f32[128,1024]{1,0:T(8,128)S(1)}) custom-call(f32[128,1024]{1,0:T(8,128)} %bitcast.13, f32[128,1024]{1,0:T(8,128)} %bitcast.14, f32[128,1024]{1,0:T(8,128)} %bitcast.15, f32[8,512]{1,0:T(8,128)} %bitcast.18, f32[8,512]{1,0:T(8,128)} %bitcast.19, s32[1,512]{1,0:T(1,128)} %cells_ref.1, f32[128,1024]{1,0:T(8,128)} %bitcast.16, ...), custom_call_target="tpu_custom_call" | custom-call | tf_op jit(solution)/shard_map/saddle/pallas_call | solution.py:746
  63.6 0.8 %copy.17 = f32[1,8,16,1024]{3,2,1,0:T(8,128)} copy(f32[1,8,16,1024]{3,2,1,0:T(8,128)S(1)} %bitcast.12) | data formatting | bytes 1048576
  64.4 0.8 %copy.18 = f32[1,8,16,1024]{3,2,1,0:T(8,128)} copy(f32[1,8,16,1024]{3,2,1,0:T(8,128)S(1)} %bitcast.11) | data formatting | bytes 1048576
